TPU v7x, 32 devices: a whole 2x2x4 slice. The times are simulated.
32 devices in a mesh: dp: 2 (over core), expert: 4 (over z), tpin: 2 (over y), tpout: 2 (over x).
Axes of the slice: x: 2, y: 2, z: 4, core: 2. Of those that a mesh axis runs over, the one named last changes fastest.
Arguments:
- tokens: bfloat16 [64, 6144], P('expert', ('dp', 'tpin', 'tpout')), may hold values from -6 to 6
- cotangent: bfloat16 [64, 6144], P('expert', ('dp', 'tpin', 'tpout')), may hold values from -6 to 6
- expert_ids: int32 [64, 2], P('expert'), may hold values from 0 to 7, all different within a row; in each aligned block of 16 rows (0 to 15, 16 to 31, ...) at most 6 rows name the same one
- gate_weights: float32 [64, 2], P('expert'), may hold values from 0.25 to 1
- w_gate: bfloat16 [6144, 65536], P(('dp', 'tpin'), ('expert', 'tpout')), may hold values from -0.078125 to 0.078125
- w_up: bfloat16 [6144, 65536], P(('dp', 'tpin'), ('expert', 'tpout')), may hold values from -0.078125 to 0.078125
- w_down: bfloat16 [65536, 6144], P(('expert', 'tpout'), ('dp', 'tpin')), may hold values from -0.0625 to 0.0625
Outputs:
- layer_out: bfloat16 [64, 6144], P('expert', ('dp', 'tpin', 'tpout'))
- token_grad: bfloat16 [64, 6144], P('expert', ('dp', 'tpin', 'tpout'))
- down_grad: bfloat16 [65536, 6144], P(('expert', 'tpout'), ('dp', 'tpin'))
Inputs may be any that keep to these rules, and one draw needn't show every extreme that they name: `expert_ids`: each row names 2 different experts. In each aligned block of 16 rows no expert is named by more than 6 rows, a bound that some block reaches.
All inputs are finite; a program needn't handle non-finite values.
Results may differ from a plain program's by a relative error of at most 0.0057.
Values may be sent and summed in bfloat16 or wider, within the bound.
No kernel may reach another device: no remote copies, remote signals or barrier semaphores. Data moves between devices by JAX's collectives and lax.ppermute only.
A program may use at most 192 MiB of HBM per device.

v0:
```python
import jax
import jax.numpy as jnp
from jax import lax
from jax.sharding import PartitionSpec as P

EXPERTS = 8
HID = 8192
CAP = 6


def contract_last(left, right):
    return lax.dot_general(
        left, right, (((1,), (1,)), ((), ())), preferred_element_type=jnp.float32
    )


def contract_first(left, right):
    return lax.dot_general(
        left,
        right,
        (((0,), (0,)), ((), ())),
        preferred_element_type=jnp.float32,
        precision=lax.Precision.HIGHEST,
    )


def swiglu_grads(gate, up, hidden_grad):
    sig = jax.nn.sigmoid(gate)
    hidden = (gate * sig * up).astype(jnp.bfloat16)
    gate_grad = (hidden_grad * up * sig * (1.0 + gate * (1.0 - sig))).astype(jnp.bfloat16)
    up_grad = (hidden_grad * gate * sig).astype(jnp.bfloat16)
    return (hidden, gate_grad, up_grad)


def per_device(tokens, cotangent, expert_ids, gate_weights, w_gate, w_up, w_down):
    expert_count = lax.axis_size("expert")
    outer_count = lax.axis_size("tpout")
    tok_rows, feat_cols = tokens.shape
    wide_cols, unit_cols = w_gate.shape
    block_w = unit_cols * outer_count
    per_block = max(1, block_w // HID)
    slot_count = per_block * CAP
    send_rows = expert_count * slot_count
    route_total = tok_rows * expert_ids.shape[1]
    flat_ids = expert_ids.reshape(route_total)
    onehot = (flat_ids[:, None] == jnp.arange(EXPERTS, dtype=jnp.int32)[None, :]).astype(jnp.int32)
    earlier = jnp.cumsum(onehot, axis=0) - onehot
    slot_rank = jnp.sum(earlier * onehot, axis=1)
    route_key = (flat_ids * CAP + slot_rank).reshape(expert_ids.shape)
    dest_index = jnp.arange(expert_count, dtype=jnp.int32)[:, None, None]
    group_index = jnp.arange(per_block, dtype=jnp.int32)[None, :, None]
    column = jnp.arange(CAP, dtype=jnp.int32)[None, None, :]
    target = ((dest_index * block_w // HID + group_index) * CAP + column).reshape(send_rows)
    route_match = route_key[None, :, :] == target[:, None, None]
    chosen = jnp.any(route_match, axis=2).astype(jnp.bfloat16)
    slot_weights = jnp.sum(jnp.where(route_match, gate_weights[None, :, :], 0.0), axis=2)
    slot_gate = jnp.sum(slot_weights, axis=1)
    x_send = jnp.dot(chosen, tokens, preferred_element_type=jnp.float32).astype(jnp.bfloat16)
    dy_pick = jnp.dot(chosen, cotangent, preferred_element_type=jnp.float32)
    dy_send = (slot_gate[:, None] * dy_pick).astype(jnp.bfloat16)
    x_recv, dy_recv = (
        lax.all_to_all(
            x_send.reshape(expert_count, slot_count, feat_cols),
            "expert",
            split_axis=0,
            concat_axis=0,
            tiled=True,
        ),
        lax.all_to_all(
            dy_send.reshape(expert_count, slot_count, feat_cols),
            "expert",
            split_axis=0,
            concat_axis=0,
            tiled=True,
        ),
    )
    x_all, dy_all = (
        lax.all_gather(x_recv, "tpout", axis=2, tiled=True),
        lax.all_gather(dy_recv, "tpout", axis=2, tiled=True),
    )
    expert_index = lax.axis_index("expert")
    outer_index = lax.axis_index("tpout")
    my_expert = (expert_index * outer_count + outer_index) * unit_cols // HID
    my_group = my_expert - expert_index * block_w // HID
    group_rows = expert_count * CAP

    def pick_group(whole):
        split = whole.reshape(expert_count, per_block, CAP, wide_cols)
        return lax.dynamic_slice_in_dim(split, my_group, 1, 1).reshape(group_rows, wide_cols)

    x_rows = pick_group(x_all)
    dy_rows = pick_group(dy_all)
    gate, up, hidden_grad = lax.psum(
        (
            jnp.dot(x_rows, w_gate, preferred_element_type=jnp.float32),
            jnp.dot(x_rows, w_up, preferred_element_type=jnp.float32),
            contract_last(dy_rows, w_down),
        ),
        ("dp", "tpin"),
    )
    hidden, gate_grad, up_grad = swiglu_grads(gate, up, hidden_grad)
    down_grad = lax.dot_general(
        hidden, dy_rows, (((0,), (0,)), ((), ())), preferred_element_type=jnp.float32
    ).astype(jnp.bfloat16)
    out_rows = jnp.dot(hidden, w_down, preferred_element_type=jnp.float32)
    grad_rows = contract_last(gate_grad, w_gate) + contract_last(up_grad, w_up)

    def widen_rows(rows):
        placed = rows.reshape(expert_count, 1, CAP, wide_cols)
        if per_block == 1:
            return placed.reshape(expert_count, slot_count, wide_cols)
        empty = jnp.zeros((expert_count, per_block, CAP, wide_cols), jnp.float32)
        return lax.dynamic_update_slice_in_dim(empty, placed, my_group, 1).reshape(
            expert_count, slot_count, wide_cols
        )

    out_back, grad_back = (
        lax.psum_scatter(widen_rows(out_rows), "tpout", scatter_dimension=2, tiled=True),
        lax.psum_scatter(widen_rows(grad_rows), "tpout", scatter_dimension=2, tiled=True),
    )
    out_home, grad_home = (
        lax.all_to_all(out_back, "expert", split_axis=0, concat_axis=0, tiled=True),
        lax.all_to_all(grad_back, "expert", split_axis=0, concat_axis=0, tiled=True),
    )
    layer_out = contract_first(slot_weights, out_home.reshape(send_rows, feat_cols)).astype(
        jnp.bfloat16
    )
    token_grad = contract_first(
        chosen.astype(jnp.float32), grad_home.reshape(send_rows, feat_cols)
    ).astype(jnp.bfloat16)
    return (layer_out, token_grad, down_grad)


def solution(mesh):
    return jax.shard_map(
        per_device,
        mesh=mesh,
        in_specs=(
            P("expert", ("dp", "tpin", "tpout")),
            P("expert", ("dp", "tpin", "tpout")),
            P("expert", None),
            P("expert", None),
            P(("dp", "tpin"), ("expert", "tpout")),
            P(("dp", "tpin"), ("expert", "tpout")),
            P(("expert", "tpout"), ("dp", "tpin")),
        ),
        out_specs=(
            P("expert", ("dp", "tpin", "tpout")),
            P("expert", ("dp", "tpin", "tpout")),
            P(("expert", "tpout"), ("dp", "tpin")),
        ),
        check_vma=False,
    )
```

profile of v0, /device:TPU:0, one launch (start us, length us, event | category | flops | bytes accessed | tf_op | source)
XLA Modules:
  0.0 260.6 jit_solution(11836724278844483289)
XLA Ops:
  7.4 0.8 copy.50
  8.8 0.7 multiply_add_fusion
  10.4 6.3 %all-to-all-start = ((bf16[4,12,768]{2,1,0:T(8,128)(2,1)}), bf16[4,12,768]{2,1,0:T(8,128)(2,1)S(1)}, u32[]{:S(2)}, u32[]{:S(2)}) async-start(bf16[4,12,768]{2,1,0:T(8,128)(2,1)} %reshape.130), calls=%async_computation | async-start | bytes 196608 | tf_op jit(solution)/shard_map/all_to_all | solution.py:62
  16.7 0.8 select_reduce_fusion
  17.5 1.0 fusion
  18.5 0.7 reshape.136
  19.1 3.4 %all-to-all-done = bf16[4,12,768]{2,1,0:T(8,128)(2,1)S(1)} async-done(((bf16[4,12,768]{2,1,0:T(8,128)(2,1)}), bf16[4,12,768]{2,1,0:T(8,128)(2,1)S(1)}, u32[]{:S(2)}, u32[]{:S(2)}) %all-to-all-start) | async-done | bytes 73760 | tf_op jit(solution)/shard_map/all_to_all | solution.py:62
  22.6 3.3 %all-to-all-start.2 = ((bf16[4,12,768]{2,1,0:T(8,128)(2,1)}), bf16[4,12,768]{2,1,0:T(8,128)(2,1)S(1)}, u32[]{:S(2)}, u32[]{:S(2)}) async-start(bf16[4,12,768]{2,1,0:T(8,128)(2,1)} %reshape.136), calls=%async_computation.2 | async-start | bytes 196608 | tf_op jit(solution)/shard_map/all_to_all | solution.py:69
  26.0 5.3 %all_gather.6 = bf16[4,12,1536]{2,1,0:T(8,128)(2,1)S(1)} all-gather(bf16[4,12,768]{2,1,0:T(8,128)(2,1)S(1)} %all-to-all-done), channel_id=1, replica_groups=mesh['dp'=2,'expert'=4,'tpin'=2,'tpout'=2] {'tpout'}, dimensions={2}, use_global_device_ids=true | all-gather | bytes 221184 | tf_op jit(solution)/shard_map/all_gather | solution.py:78
  31.7 5.3 %all_gather.7 = bf16[4,12,1536]{2,1,0:T(8,128)(2,1)S(1)} all-gather(bf16[4,12,768]{2,1,0:T(8,128)(2,1)S(1)} %all-to-all-done.2), channel_id=1, replica_groups=mesh['dp'=2,'expert'=4,'tpin'=2,'tpout'=2] {'tpout'}, dimensions={2}, use_global_device_ids=true | all-gather | bytes 221184 | tf_op jit(solution)/shard_map/all_gather | solution.py:79
  37.3 10.8 %fusion.8 = f32[24,8192]{1,0:T(8,128)} fusion(bf16[24,1536]{1,0:T(8,128)(2,1)S(1)} %reshape.132, bf16[1536,8192]{1,0:T(8,128)(2,1)} %param.12), kind=kOutput, calls=%fused_computation.34 | convolution fusion | flops 603979776 | bytes 26025984 | tf_op jit(solution)/shard_map/dot_general | solution.py:96
  48.1 10.8 %fusion.7 = f32[24,8192]{1,0:T(8,128)} fusion(bf16[24,1536]{1,0:T(8,128)(2,1)S(1)} %reshape.132, bf16[1536,8192]{1,0:T(8,128)(2,1)} %param.11), kind=kOutput, calls=%fused_computation.33 | convolution fusion | flops 603979776 | bytes 26025984 | tf_op jit(solution)/shard_map/dot_general | solution.py:95
  58.9 12.4 %fusion.10 = f32[24,8192]{1,0:T(8,128)} fusion(bf16[24,1536]{1,0:T(8,128)(2,1)S(1)} %reshape.138, bf16[8192,1536]{1,0:T(8,128)(2,1)} %param.13), kind=kOutput, calls=%fused_computation.36 | convolution fusion | flops 603979776 | bytes 26025984 | tf_op jit(solution)/shard_map/dot_general | solution.py:12
  71.5 57.0 %all-reduce.3.cloned.1.call-done = (f32[24,8192]{1,0:T(8,128)}, f32[24,8192]{1,0:T(8,128)}, f32[24,8192]{1,0:T(8,128)}) async-done(((f32[24,8192]{1,0:T(8,128)}, f32[24,8192]{1,0:T(8,128)}, f32[24,8192]{1,0:T(8,128)}), (f32[24,8192]{1,0:T(8,128)}, f32[24,8192]{1,0:T(8,128)}, f32[24,8192]{1,0:T(8,128)})) %all-reduce.3.cloned.1.call-update) | async-done | bytes 2359312 | tf_op jit(solution)/shard_map/psum | solution.py:93
  128.6 1.6 multiply_convert_fusion.2
  130.2 15.4 %fusion.1 = f32[24,1536]{1,0:T(8,128)S(1)} fusion(bf16[1536,8192]{1,0:T(8,128)(2,1)} %param.11, f32[24,8192]{1,0:T(8,128)} %get-tuple-element.6, f32[24,8192]{1,0:T(8,128)} %get-tuple-element.7, f32[24,8192]{1,0:T(8,128)} %get-tuple-element.5), kind=kOutput, calls=%fused_computation.11 | convolution fusion | flops 605945856 | bytes 27672576 | tf_op jit(solution)/shard_map/dot_general | solution.py:12
  145.6 11.6 %convolution_add_fusion = f32[24,1536]{1,0:T(8,128)S(1)} fusion(f32[24,1536]{1,0:T(8,128)S(1)} %fusion.1, bf16[1536,8192]{1,0:T(8,128)(2,1)} %param.12, f32[24,8192]{1,0:T(8,128)S(1)} %copy-done.3, f32[24,8192]{1,0:T(8,128)S(1)} %copy-done.2), kind=kOutput, calls=%fused_computation.1 | convolution fusion | flops 605196288 | bytes 27033600 | tf_op jit(solution)/shard_map/dot_general | solution.py:12
  157.4 8.2 %copy.62 = f32[4,12,1536]{0,1,2:T(8,128)} copy(f32[4,12,1536]{2,0,1:T(4,128)S(1)} %bitcast.39) | data formatting | bytes 589824
  165.6 9.0 %reshape.144 = f32[1536,48]{1,0:T(8,128)} reshape(f32[1536,12,4]{2,1,0:T(8,128)} %bitcast.34) | data formatting | bytes 589824
  174.8 10.2 %fusion.9 = f32[24,1536]{1,0:T(8,128)S(1)} fusion(bf16[24,8192]{1,0:T(8,128)(2,1)S(1)} %multiply_convert_fusion.2, bf16[8192,1536]{1,0:T(8,128)(2,1)} %param.13), kind=kOutput, calls=%fused_computation.35 | convolution fusion | flops 603979776 | bytes 25706496 | tf_op jit(solution)/shard_map/dot_general | solution.py:105
  185.2 8.2 %copy.60 = f32[4,12,1536]{0,1,2:T(8,128)} copy(f32[4,12,1536]{2,0,1:T(4,128)S(1)} %bitcast.38) | data formatting | bytes 589824
  193.4 9.0 %reshape.142 = f32[1536,48]{1,0:T(8,128)} reshape(f32[1536,12,4]{2,1,0:T(8,128)} %bitcast.35) | data formatting | bytes 589824
  202.4 5.2 %reshape.145 = f32[768,12,4]{2,1,0:T(8,128)} reshape(f32[768,48]{1,0:T(8,128)} %reduce-scatter.9.cloned.1.call-done) | data formatting | bytes 294912
  207.6 6.1 %copy.59 = f32[4,12,768]{2,1,0:T(8,128)} copy(f32[4,12,768]{0,1,2:T(8,128)} %bitcast.36) | data formatting | bytes 294912 | tf_op jit(solution)/shard_map/reduce_scatter | solution.py:119
  213.7 4.5 %all-to-all-start.3 = ((f32[4,12,768]{2,1,0:T(8,128)}), f32[4,12,768]{2,1,0:T(8,128)S(1)}, u32[]{:S(2)}, u32[]{:S(2)}) async-start(f32[4,12,768]{2,1,0:T(8,128)} %copy.59), calls=%async_computation.3 | async-start | bytes 393216 | tf_op jit(solution)/shard_map/all_to_all | solution.py:123
  218.2 12.4 %convolution_convert_fusion = bf16[8192,1536]{1,0:T(8,128)(2,1)} fusion(bf16[24,8192]{1,0:T(8,128)(2,1)S(1)} %multiply_convert_fusion.2, bf16[24,1536]{1,0:T(8,128)(2,1)S(1)} %reshape.138), kind=kOutput, calls=%fused_computation | convolution fusion | flops 616562688 | bytes 25632768 | tf_op jit(solution)/shard_map/dot_general | solution.py:102
  230.6 5.2 %reshape.143 = f32[768,12,4]{2,1,0:T(8,128)} reshape(f32[768,48]{1,0:T(8,128)} %reduce-scatter.7.cloned.1.call-done) | data formatting | bytes 294912
  235.8 5.8 %copy.55 = f32[4,12,768]{2,1,0:T(8,128)} copy(f32[4,12,768]{0,1,2:T(8,128)} %bitcast.37) | data formatting | bytes 294912 | tf_op jit(solution)/shard_map/reduce_scatter | solution.py:118
  241.6 5.1 %all-to-all-start.1 = ((f32[4,12,768]{2,1,0:T(8,128)}), f32[4,12,768]{2,1,0:T(8,128)S(1)}, u32[]{:S(2)}, u32[]{:S(2)}) async-start(f32[4,12,768]{2,1,0:T(8,128)} %copy.55), calls=%async_computation.1 | async-start | bytes 393216 | tf_op jit(solution)/shard_map/all_to_all | solution.py:122
  246.7 0.8 convolution_convert_fusion.2
  247.5 5.7 %all-to-all-done.1 = f32[4,12,768]{2,1,0:T(8,128)S(1)} async-done(((f32[4,12,768]{2,1,0:T(8,128)}), f32[4,12,768]{2,1,0:T(8,128)S(1)}, u32[]{:S(2)}, u32[]{:S(2)}) %all-to-all-start.1) | async-done | bytes 147488 | tf_op jit(solution)/shard_map/all_to_all | solution.py:122
  253.2 0.8 convolution_convert_fusion.3
  (46 shorter events, 3.5 us)
Async XLA Ops:
  7.2 2.4 copy-start
  10.4 12.2 %all-to-all-start = ((bf16[4,12,768]{2,1,0:T(8,128)(2,1)}), bf16[4,12,768]{2,1,0:T(8,128)(2,1)S(1)}, u32[]{:S(2)}, u32[]{:S(2)}) async-start(bf16[4,12,768]{2,1,0:T(8,128)(2,1)} %reshape.130), calls=%async_computation | async-start | bytes 196608 | tf_op jit(solution)/shard_map/all_to_all | solution.py:62
  22.6 9.1 %all-to-all-start.2 = ((bf16[4,12,768]{2,1,0:T(8,128)(2,1)}), bf16[4,12,768]{2,1,0:T(8,128)(2,1)S(1)}, u32[]{:S(2)}, u32[]{:S(2)}) async-start(bf16[4,12,768]{2,1,0:T(8,128)(2,1)} %reshape.136), calls=%async_computation.2 | async-start | bytes 196608 | tf_op jit(solution)/shard_map/all_to_all | solution.py:69
  25.9 102.7 %all-reduce.3.cloned.1.call-start = ((), (), s32[]{:S(2)}) async-start(), calls=%async_computation.8 | async-start | bytes 4718592 | tf_op jit(solution)/shard_map/psum | solution.py:93
  71.3 131.1 %reduce-scatter.9.cloned.1.call-start = ((), (), s32[]{:S(2)}) async-start(), calls=%async_computation.7 | async-start | bytes 1179648
  130.1 15.4 %copy-start.2 = (f32[24,8192]{1,0:T(8,128)S(1)}, f32[24,8192]{1,0:T(8,128)}, u32[]{:S(2)}) copy-start(f32[24,8192]{1,0:T(8,128)} %get-tuple-element.6) | copy-start | bytes 2359300
  130.2 15.4 %copy-start.3 = (f32[24,8192]{1,0:T(8,128)S(1)}, f32[24,8192]{1,0:T(8,128)}, u32[]{:S(2)}) copy-start(f32[24,8192]{1,0:T(8,128)} %get-tuple-element.7) | copy-start | bytes 2359300
  174.6 56.0 %reduce-scatter.7.cloned.1.call-start = ((), (), s32[]{:S(2)}) async-start(), calls=%async_computation.6 | async-start | bytes 1179648
  213.7 27.9 %all-to-all-start.3 = ((f32[4,12,768]{2,1,0:T(8,128)}), f32[4,12,768]{2,1,0:T(8,128)S(1)}, u32[]{:S(2)}, u32[]{:S(2)}) async-start(f32[4,12,768]{2,1,0:T(8,128)} %copy.59), calls=%async_computation.3 | async-start | bytes 393216 | tf_op jit(solution)/shard_map/all_to_all | solution.py:123
  218.2 35.9 %copy-start.1 = (bf16[16,768]{1,0:T(8,128)(2,1)S(1)}, bf16[16,768]{1,0:T(8,128)(2,1)}, u32[]{:S(2)}) copy-start(bf16[16,768]{1,0:T(8,128)(2,1)} %param.7) | copy-start | bytes 73732
  241.6 11.6 %all-to-all-start.1 = ((f32[4,12,768]{2,1,0:T(8,128)}), f32[4,12,768]{2,1,0:T(8,128)S(1)}, u32[]{:S(2)}, u32[]{:S(2)}) async-start(f32[4,12,768]{2,1,0:T(8,128)} %copy.55), calls=%async_computation.1 | async-start | bytes 393216 | tf_op jit(solution)/shard_map/all_to_all | solution.py:122
Sparse Core Ops, SparseCore 0:
  71.4 57.0 all-reduce.2
  174.7 17.4 reduce-scatter.8
  202.5 17.4 reduce-scatter.6
where the time goes:
time: 262 us; the launch traced here: 261 us
  matrix products  86.3 us (33%)
  waiting for transfers between devices  66.5 us (25%)
  local copies, waits for them, and re-layouts  59.8 us (23%)
  starting transfers between devices  19.7 us (8%)
  between operations  14 us (5%)
  blocking collectives  10.6 us (4%)
  other arithmetic  3.59 us (1%)
    psum x1, waiting for transfers between devices, per_device(): lax.psum((jnp.dot(x_rows, w_gate, preferred_element_type=jnp.float32), jn...  57 us
    unnamed x15, local copies, waits for them, and re-layouts  45.5 us
    dot_general x3, matrix products, contract_last(): lax.dot_general(left, right, (((1,), (1,)), ((), ())), preferred_element_...  39.4 us
    dot_general x1, matrix products, per_device(): lax.dot_general(hidden, dy_rows, (((0,), (0,)), ((), ())), preferred_elem...  12.4 us
    dot_general x1, matrix products, per_device(): jnp.dot(x_rows, w_up, preferred_element_type=jnp.float32)  10.8 us
    dot_general x1, matrix products, per_device(): jnp.dot(x_rows, w_gate, preferred_element_type=jnp.float32)  10.8 us
    dot_general x1, matrix products, per_device(): out_rows = jnp.dot(hidden, w_down, preferred_element_type=jnp.float32)  10.2 us
    all_to_all x1, starting transfers between devices, per_device(): lax.all_to_all(x_send.reshape(expert_count, slot_count, feat_cols), 'expe...  6.32 us
  transfers between devices with their start and end apart: 7, of which 4 were waited for; matrix products, arithmetic and copies ran while one was open for 25% of the time, Pallas kernels for 0%

commit v1 on v0

v1 whole, which is shorter than its diff:
```python
import math

import jax
import jax.numpy as jnp
import numpy as np
from jax import lax
from jax.experimental import pallas as pl
from jax.experimental.pallas import tpu as pltpu
from jax.sharding import PartitionSpec as P

EXPERTS = 8
HID = 8192
CAP = 6
SLAB = 16
ROUTE_AXES = ("tpout", "expert")

NN = (((1,), (0,)), ((), ()))
NT = (((1,), (1,)), ((), ()))
TN = (((0,), (0,)), ((), ()))
VMEM = pl.BlockSpec(memory_space=pltpu.VMEM)
ANY = pl.BlockSpec(memory_space=pl.ANY)


def dot(left, right, dims=NN, precision=None):
    return lax.dot_general(
        left, right, dims, preferred_element_type=jnp.float32, precision=precision
    )


def params():
    return pltpu.CompilerParams(vmem_limit_bytes=44 << 20)


def cost(flops, nbytes):
    return pl.CostEstimate(flops=int(flops), bytes_accessed=int(nbytes), transcendentals=0)


def route_rows(tokens, cotangent, expert_ids, gate_weights, dest_expert):
    tok_rows, feat = tokens.shape
    rows = len(dest_expert) * SLAB
    j = np.arange(rows) % SLAB
    slot = np.where(j < 2 * CAP, j % CAP, -1)
    table = np.stack([np.repeat(np.asarray(dest_expert), SLAB), slot, (j < CAP) * 1, j * 0], 1)
    first = np.zeros((2, rows, expert_ids.shape[1]), np.float32)
    first[0, :, 0] = 1
    first[1, :, 1] = 1
    before = np.triu(np.ones((tok_rows, tok_rows), np.float32), 1)

    def kernel(tok, cot, ids, gw, tab, one, bef, send, home):
        want = tab[:, 0:1].astype(jnp.float32)
        slot = tab[:, 1:2].astype(jnp.float32)
        is_x = tab[:, 2:3] == 1
        fid = ids[...].astype(jnp.float32)
        hit = jnp.zeros((rows, tok_rows), jnp.bool_)
        weight = jnp.zeros((rows, tok_rows), jnp.float32)
        for k in range(2):
            same = dot(one[k], fid, NT) == want
            hit = hit | same
            weight += jnp.where(same, dot(one[k], gw[...], NT, lax.Precision.HIGHEST), 0.0)
        rank = dot(hit.astype(jnp.float32), bef[...])
        chosen = jnp.where(hit & (rank == slot), 1.0, 0.0)
        pick = chosen.astype(jnp.bfloat16)
        row_weight = jnp.sum(chosen * weight, axis=1, keepdims=True)
        x = dot(pick, tok[...])
        dy = row_weight * dot(pick, cot[...])
        send[...] = jnp.where(is_x, x, dy).astype(jnp.bfloat16)
        home[...] = jnp.where(is_x, chosen * weight, chosen)

    return pl.pallas_call(
        kernel,
        in_specs=[VMEM] * 7,
        out_specs=[VMEM] * 2,
        out_shape=[
            jax.ShapeDtypeStruct((rows, feat), jnp.bfloat16),
            jax.ShapeDtypeStruct((rows, tok_rows), jnp.float32),
        ],
        compiler_params=params(),
        name="route_rows",
    )(
        tokens,
        cotangent,
        expert_ids,
        gate_weights,
        jnp.asarray(table, jnp.int32),
        jnp.asarray(first),
        jnp.asarray(before),
    )


def combine_rows(back, home, tok_rows):
    rows, feat = back.shape

    def kernel(b, h, out, grad):
        j = lax.broadcasted_iota(jnp.int32, h.shape, 0) % SLAB
        vals = b[...].astype(jnp.float32)
        for_out = jnp.where(j < CAP, h[...], 0.0)
        for_grad = jnp.where(j < CAP, 0.0, h[...])
        out[...] = dot(for_out, vals, TN, lax.Precision.HIGHEST).astype(jnp.bfloat16)
        grad[...] = dot(for_grad.astype(jnp.bfloat16), b[...], TN).astype(jnp.bfloat16)

    shape = jax.ShapeDtypeStruct((tok_rows, feat), jnp.bfloat16)
    return pl.pallas_call(
        kernel,
        in_specs=[VMEM] * 2,
        out_specs=[VMEM] * 2,
        out_shape=[shape, shape],
        compiler_params=params(),
        name="combine_rows",
    )(back, home)


class Stream:
    def __init__(self, sources, slots, sems, base, width, steps):
        self.sources, self.slots, self.sems = sources, slots, sems
        self.base, self.width, self.steps = base, width, steps
        self.depth = slots[0].shape[0]

    def copies(self, step):
        at = pl.ds(self.base + step * self.width, self.width)
        slot = step % self.depth
        gate, up, down = self.sources
        views = (gate.at[:, at], up.at[:, at], down.at[at, :])
        return [
            pltpu.make_async_copy(view, held.at[slot], self.sems.at[i, slot])
            for i, (view, held) in enumerate(zip(views, self.slots))
        ]

    def open(self):
        for step in range(min(self.depth, self.steps)):
            for copy in self.copies(step):
                copy.start()

    def take(self, step):
        for copy in self.copies(step):
            copy.wait()
        return [held.at[step % self.depth] for held in self.slots]

    def done(self, step):
        if step + self.depth < self.steps:
            for copy in self.copies(step + self.depth):
                copy.start()


def stream_scratch(wide, width, depth):
    return [
        pltpu.VMEM((depth, wide, width), jnp.bfloat16),
        pltpu.VMEM((depth, wide, width), jnp.bfloat16),
        pltpu.VMEM((depth, width, wide), jnp.bfloat16),
        pltpu.SemaphoreType.DMA((3, depth)),
    ]


def block_width(cols):
    width = min(512, cols)
    depth = min(4, cols // width)
    return width, depth


def spread(recv_rows, expert_count, outer_count, x_all, dy_all, recv):
    feat = recv.shape[1]
    slabs = expert_count * SLAB
    r = lax.broadcasted_iota(jnp.int32, (recv_rows, slabs), 0)
    c = lax.broadcasted_iota(jnp.int32, (recv_rows, slabs), 1)
    place = (r // CAP) * SLAB + r % CAP
    for_x = jnp.where(c == place, 1.0, 0.0).astype(jnp.bfloat16)
    for_dy = jnp.where(c == place + CAP, 1.0, 0.0).astype(jnp.bfloat16)
    for o in range(outer_count):
        part = recv[o * slabs : (o + 1) * slabs, :]
        x_all[:, o * feat : (o + 1) * feat] = dot(for_x, part).astype(jnp.bfloat16)
        dy_all[:, o * feat : (o + 1) * feat] = dot(for_dy, part).astype(jnp.bfloat16)


def first_phase(rows_in, w_gate, w_up, w_down, base, cols, counts):
    wide = w_gate.shape[0]
    rows = counts[0] * CAP
    width, depth = block_width(cols)
    steps = cols // width
    opening = len(rows_in) == 1

    def kernel(*refs):
        refs = list(refs)
        rows_refs = [refs.pop(0) for _ in rows_in]
        sources = [refs.pop(0) for _ in range(3)]
        if opening:
            exact, rounded, x_all, dy_all = refs[:4]
            refs = refs[4:]
        else:
            exact, rounded = refs[:2]
            refs = refs[2:]
            x_all, dy_all = rows_refs
        stream = Stream(sources, refs[:3], refs[3], base, width, steps)
        stream.open()
        if opening:
            spread(rows, counts[0], counts[1], x_all, dy_all, rows_refs[0])
        for step in range(steps):
            gate, up, down = stream.take(step)
            at = step * width
            parts = (
                dot(x_all[...], gate[...]),
                dot(x_all[...], up[...]),
                dot(dy_all[...], down[...], NT),
            )
            for i, part in enumerate(parts):
                exact[:, i * cols + at : i * cols + at + width] = part
                rounded[:, i * cols + at : i * cols + at + width] = part.astype(jnp.bfloat16)
            stream.done(step)

    shapes = [
        jax.ShapeDtypeStruct((rows, 3 * cols), jnp.float32),
        jax.ShapeDtypeStruct((rows, 3 * cols), jnp.bfloat16),
    ]
    if opening:
        shapes += [jax.ShapeDtypeStruct((rows, wide), jnp.bfloat16)] * 2
    return pl.pallas_call(
        kernel,
        in_specs=[VMEM] * len(rows_in) + [ANY] * 3,
        out_specs=[VMEM] * len(shapes),
        out_shape=shapes,
        scratch_shapes=stream_scratch(wide, width, depth),
        compiler_params=params(),
        cost_estimate=cost(6 * 256 * wide * cols, 6 * wide * cols),
        name="first_phase",
    )(*rows_in, w_gate, w_up, w_down)


def second_phase(parts, sums, w_gate, w_up, w_down, base, cols, counts, last):
    wide = w_gate.shape[0]
    rows = counts[0] * CAP
    feat = wide // counts[1]
    slabs = counts[0] * SLAB
    width, depth = block_width(cols)
    steps = cols // width

    def kernel(*refs):
        refs = list(refs)
        part_refs = [refs.pop(0) for _ in parts]
        sum_refs = [refs.pop(0) for _ in sums]
        sources = [refs.pop(0) for _ in range(3)]
        hidden = refs.pop(0)
        outs = [refs.pop(0) for _ in range(1 if last else 2)]
        slots, sems = refs[:3], refs[3]
        gate_grad, up_grad = refs[4:6]
        acc = refs[6:8] if last else outs
        stream = Stream(sources, slots, sems, base, width, steps)
        stream.open()
        for step in range(steps):
            at = step * width
            gate, up, hidden_grad = [
                sum(p[:, i * cols + at : i * cols + at + width] for p in part_refs)
                for i in range(3)
            ]
            sig = 1.0 / (1.0 + jnp.exp(-gate))
            act = gate * sig
            here = slice(at, at + width)
            hidden[:, here] = (act * up).astype(jnp.bfloat16)
            gate_grad[:, here] = (
                hidden_grad * up * sig * (1.0 + gate * (1.0 - sig))
            ).astype(jnp.bfloat16)
            up_grad[:, here] = (hidden_grad * act).astype(jnp.bfloat16)
        for step in range(steps):
            w_g, w_u, w_d = stream.take(step)
            here = slice(step * width, (step + 1) * width)
            out = dot(hidden[:, here], w_d[...])
            grad = dot(gate_grad[:, here], w_g[...], NT) + dot(up_grad[:, here], w_u[...], NT)
            if step == 0 and not sums:
                acc[0][...] = out
                acc[1][...] = grad
            elif step == 0:
                acc[0][...] = sum_refs[0][...] + out
                acc[1][...] = sum_refs[1][...] + grad
            else:
                acc[0][...] += out
                acc[1][...] += grad
            stream.done(step)
        if last:
            r = lax.broadcasted_iota(jnp.int32, (slabs, rows), 0)
            c = lax.broadcasted_iota(jnp.int32, (slabs, rows), 1)
            place = (c // CAP) * SLAB + c % CAP
            from_out = jnp.where(r == place, 1.0, 0.0).astype(jnp.bfloat16)
            from_grad = jnp.where(r == place + CAP, 1.0, 0.0).astype(jnp.bfloat16)
            out16 = acc[0][...].astype(jnp.bfloat16)
            grad16 = acc[1][...].astype(jnp.bfloat16)
            for o in range(counts[1]):
                cut = slice(o * feat, (o + 1) * feat)
                outs[0][o * slabs : (o + 1) * slabs, :] = (
                    dot(from_out, out16[:, cut]) + dot(from_grad, grad16[:, cut])
                ).astype(jnp.bfloat16)

    scratch = stream_scratch(wide, width, depth)
    scratch += [pltpu.VMEM((rows, cols), jnp.bfloat16)] * 2
    shapes = [jax.ShapeDtypeStruct((rows, cols), jnp.bfloat16)]
    if last:
        scratch += [pltpu.VMEM((rows, wide), jnp.float32)] * 2
        shapes += [jax.ShapeDtypeStruct((counts[1] * slabs, feat), jnp.bfloat16)]
    else:
        shapes += [jax.ShapeDtypeStruct((rows, wide), jnp.float32)] * 2
    return pl.pallas_call(
        kernel,
        in_specs=[VMEM] * (len(parts) + len(sums)) + [ANY] * 3,
        out_specs=[VMEM] * len(shapes),
        out_shape=shapes,
        scratch_shapes=scratch,
        compiler_params=params(),
        cost_estimate=cost(6 * 256 * wide * cols, 6 * wide * cols),
        name="second_phase",
    )(*parts, *sums, w_gate, w_up, w_down)


def outer_products(hiddens, dy_all):
    rows, wide = dy_all.shape
    cols = hiddens[0].shape[1]
    width = min(512, cols)
    per = cols // width
    total = per * len(hiddens)
    depth = min(4, total)

    def kernel(*refs):
        hidden_refs, (dy, out, held, sems) = refs[: len(hiddens)], refs[len(hiddens) :]

        def copy(step):
            return pltpu.make_async_copy(
                held.at[step % depth], out.at[pl.ds(step * width, width), :], sems.at[step % depth]
            )

        for step in range(total):
            if step >= depth:
                copy(step - depth).wait()
            at = (step % per) * width
            block = hidden_refs[step // per][:, at : at + width]
            held[step % depth] = dot(block, dy[...], TN).astype(jnp.bfloat16)
            copy(step).start()
        for step in range(total - depth, total):
            copy(step).wait()

    return pl.pallas_call(
        kernel,
        in_specs=[VMEM] * (len(hiddens) + 1),
        out_specs=ANY,
        out_shape=jax.ShapeDtypeStruct((cols * len(hiddens), wide), jnp.bfloat16),
        scratch_shapes=[
            pltpu.VMEM((depth, width, wide), jnp.bfloat16),
            pltpu.SemaphoreType.DMA((depth,)),
        ],
        compiler_params=params(),
        cost_estimate=cost(2 * 256 * wide * cols * len(hiddens), 2 * wide * cols * len(hiddens)),
        name="outer_products",
    )(*hiddens, dy_all)


def from_peers(value, axis):
    size = lax.axis_size(axis)
    return [
        lax.ppermute(value, axis, [(i, (i + hop) % size) for i in range(size)])
        for hop in range(1, size)
    ]


def per_device(tokens, cotangent, expert_ids, gate_weights, w_gate, w_up, w_down):
    expert_count = lax.axis_size("expert")
    outer_count = lax.axis_size("tpout")
    counts = (expert_count, outer_count)
    tok_rows, feat = tokens.shape
    unit_cols = w_gate.shape[1]
    dest_expert = [
        (i * outer_count + o) * unit_cols // HID
        for o in range(outer_count)
        for i in range(expert_count)
    ]
    send, home = route_rows(tokens, cotangent, expert_ids, gate_weights, dest_expert)

    def exchange(rows):
        cut = rows.reshape(outer_count * expert_count, SLAB, feat)
        return lax.all_to_all(cut, ROUTE_AXES, 0, 0, tiled=True).reshape(rows.shape)

    rows_in = (exchange(send),)
    chunks = 2 if unit_cols % 1024 == 0 else 1
    cols = unit_cols // chunks
    firsts = []
    for chunk in range(chunks):
        exact, rounded, *opened = first_phase(
            rows_in, w_gate, w_up, w_down, chunk * cols, cols, counts
        )
        if opened:
            rows_in = tuple(opened)
        firsts.append((exact, from_peers(rounded, "tpin")))
    dy_all = rows_in[1]
    sums, hiddens = (), []
    for chunk, (exact, others) in enumerate(firsts):
        mine = exact + sum(o.astype(jnp.float32) for o in others)
        parts = [mine] + from_peers(mine, "dp")
        last = chunk == chunks - 1
        hidden, *sums = second_phase(
            parts, sums, w_gate, w_up, w_down, chunk * cols, cols, counts, last
        )
        hiddens.append(hidden)
    back = exchange(sums[0])
    down_grad = outer_products(hiddens, dy_all)
    layer_out, token_grad = combine_rows(back, home, tok_rows)
    return layer_out, token_grad, down_grad


def solution(mesh):
    wide = P("expert", ("dp", "tpin", "tpout"))
    rows = P("expert", None)
    into = P(("dp", "tpin"), ("expert", "tpout"))
    out_of = P(("expert", "tpout"), ("dp", "tpin"))
    return jax.shard_map(
        per_device,
        mesh=mesh,
        in_specs=(wide, wide, rows, rows, into, into, out_of),
        out_specs=(wide, wide, out_of),
        check_vma=False,
    )
```

time: 262 us -> 107 us (0.41)
  matrix products: 86.3 us -> 0 us
  Pallas kernels: 0 us -> 66.6 us
  waiting for transfers between devices: 66.5 us -> 12.1 us
  local copies, waits for them, and re-layouts: 59.8 us -> 5.42 us
  starting transfers between devices: 19.7 us -> 5.7 us
  between operations: 14 us -> 0.74 us
  blocking collectives: 10.6 us -> 15.8 us
  other arithmetic: 3.59 us -> 0.19 us
    dot_general x11 -> x0, matrix products: 86.3 us -> none  [the longest x3 39.4 us: contract_last(): lax.dot_general(left, right, (((1,), (1,)), ((), ())), preferred_element_...]
    pallas_call x0 -> x7, Pallas kernels: none -> 66.6 us  [the longest x2 28.1 us: second_phase(): pl.pallas_call(kernel, in_specs=[VMEM] * (len(parts) + len(sums)) + [ANY]...]
    psum x1 -> x0, waiting for transfers between devices: 57 us -> none  [per_device(): lax.psum((jnp.dot(x_rows, w_gate, preferred_element_type=jnp.float32), jn...]
    unnamed x15 -> x12, local copies, waits for them, and re-layouts: 45.5 us -> 5.42 us
    all_to_all x4 -> x1, starting transfers between devices: 19.2 us -> 3.4 us  [exchange(): return lax.all_to_all(cut, ROUTE_AXES, 0, 0, tiled=True).reshape(rows.shape)]
    all_to_all x0 -> x1, blocking collectives: none -> 15.8 us  [exchange(): return lax.all_to_all(cut, ROUTE_AXES, 0, 0, tiled=True).reshape(rows.shape)]
    ppermute x0 -> x4, waiting for transfers between devices: none -> 12.1 us  [from_peers(): lax.ppermute(value, axis, [(i, (i + hop) % size) for i in range(size)])]
    reduce_scatter x2 -> x0, local copies, waits for them, and re-layouts: 11.8 us -> none  [the longest x1 6.06 us: per_device(): lax.psum_scatter(widen_rows(grad_rows), 'tpout', scatter_dimension=2, til...]
  transfers between devices with their start and end apart: 7 -> 5, of which waited for: 4 -> 1; matrix products, arithmetic and copies ran while one was open for 25% -> 0% of each run, Pallas kernels for 0% -> 35%
where the time goes in v1:
time: 107 us
  Pallas kernels  66.6 us (62%)
  blocking collectives  15.8 us (15%)
  waiting for transfers between devices  12.1 us (11%)
  starting transfers between devices  5.7 us (5%)
  local copies, waits for them, and re-layouts  5.42 us (5%)
    pallas_call x2, Pallas kernels, second_phase(): pl.pallas_call(kernel, in_specs=[VMEM] * (len(parts) + len(sums)) + [ANY]...  28.1 us
    pallas_call x2, Pallas kernels, first_phase(): pl.pallas_call(kernel, in_specs=[VMEM] * len(rows_in) + [ANY] * 3, out_sp...  26.9 us
    all_to_all x1, blocking collectives, exchange(): return lax.all_to_all(cut, ROUTE_AXES, 0, 0, tiled=True).reshape(rows.shape)  15.8 us
    ppermute x4, waiting for transfers between devices, from_peers(): lax.ppermute(value, axis, [(i, (i + hop) % size) for i in range(size)])  12.1 us
    pallas_call x1, Pallas kernels, outer_products(): pl.pallas_call(kernel, in_specs=[VMEM] * (len(hiddens) + 1), out_specs=AN...  10.2 us
    unnamed x12, local copies, waits for them, and re-layouts  5.42 us
    all_to_all x1, starting transfers between devices, exchange(): return lax.all_to_all(cut, ROUTE_AXES, 0, 0, tiled=True).reshape(rows.shape)  3.4 us
    ppermute x4, starting transfers between devices, from_peers(): lax.ppermute(value, axis, [(i, (i + hop) % size) for i in range(size)])  2.3 us
  transfers between devices with their start and end apart: 5, of which 1 were waited for; matrix products, arithmetic and copies ran while one was open for 0% of the time, Pallas kernels for 35%

profile of v1, /device:TPU:0, one launch (start us, length us, event | category | flops | bytes accessed | tf_op | source)
XLA Modules:
  0.0 106.6 jit_solution(11526281109681343026)
XLA Ops:
  0.6 0.8 copy.13.ids
  1.4 0.8 copy.14.gw
  2.1 0.0 copy-start
  2.1 0.9 copy-done
  3.0 0.0 copy-start.1
  3.0 0.8 copy-done.1
  3.9 0.0 copy-start.2
  3.9 0.7 copy-done.2
  4.6 0.0 copy-start.3
  4.6 0.7 copy-done.3
  5.4 0.0 copy-start.4
  5.4 0.7 copy-done.4
  6.1 0.5 route_rows.1
  6.6 15.8 %all_to_all.10 = bf16[8,16,768]{2,1,0:T(8,128)(2,1)S(1)} all-to-all(bf16[8,16,768]{2,1,0:T(8,128)(2,1)S(1)} %bitcast.6), channel_id=1, replica_groups=mesh['dp'=2,'expert'=4,'tpin'=2,'tpout'=2] {'tpout','expert'}, dimensions={0} | all-to-all | bytes 393216 | tf_op jit(solution)/shard_map/all_to_all | solution.py:373
  22.4 13.5 %first_phase.2 = (f32[24,12288]{1,0:T(8,128)S(1)}, bf16[24,12288]{1,0:T(8,128)(2,1)S(1)}, bf16[24,1536]{1,0:T(8,128)(2,1)S(1)}, bf16[24,1536]{1,0:T(8,128)(2,1)S(1)}) custom-call(bf16[128,768]{1,0:T(8,128)(2,1)S(1)} %bitcast.5, bf16[1536,8192]{1,0:T(8,128)(2,1)} %refs_4_.5, bf16[1536,8192]{1,0:T(8,128)(2,1)} %refs_5_.1, bf16[8192,1536]{1,0:T(8,128)(2,1)} %refs_6_.1), custom_call_target="tpu_custom_call" | custom-call | flops 9663676416 | bytes 37748736 | tf_op jit(solution)/shard_map/first_phase/pallas_call | solution.py:214
  35.8 1.6 %collective-permute-start.2 = (bf16[24,12288]{1,0:T(8,128)(2,1)S(1)}, bf16[24,12288]{1,0:T(8,128)(2,1)S(1)}, u32[]{:S(2)}, u32[]{:S(2)}) collective-permute-start(bf16[24,12288]{1,0:T(8,128)(2,1)S(1)} %get-tuple-element.24), channel_id=1, source_target_pairs={{0,2},{2,0},{1,3},{3,1},{4,6},{6,4},{5,7},{7,5},{8,10},{10,8},{9,1... | collective-permute-start | bytes 1769480 | tf_op jit(solution)/shard_map/ppermute | solution.py:353
  37.4 13.4 %first_phase.3 = (f32[24,12288]{1,0:T(8,128)S(1)}, bf16[24,12288]{1,0:T(8,128)(2,1)S(1)}) custom-call(bf16[24,1536]{1,0:T(8,128)(2,1)S(1)} %get-tuple-element.19.refs_0_, bf16[24,1536]{1,0:T(8,128)(2,1)S(1)} %get-tuple-element.20.refs_1_.refs_2_, bf16[1536,8192]{1,0:T(8,128)(2,1)} %refs_4_.5, bf16[1536,8192]{1,0:T(8,128)(2,1)} %refs_5_.1, ...), custom_call_target="tpu_custom_call" | custom-call | flops 9663676416 | bytes 37748736 | tf_op jit(solution)/shard_map/first_phase/pallas_call | solution.py:214
  50.8 0.6 collective-permute-start
  51.4 0.0 collective-permute-done.2
  51.4 0.1 convert_add_fusion.refs_0_
  51.5 0.1 collective-permute-start.3
  51.6 12.1 %collective-permute-done = bf16[24,12288]{1,0:T(8,128)(2,1)S(1)} collective-permute-done((bf16[24,12288]{1,0:T(8,128)(2,1)S(1)}, bf16[24,12288]{1,0:T(8,128)(2,1)S(1)}, u32[]{:S(2)}, u32[]{:S(2)}) %collective-permute-start) | collective-permute-done | bytes 589856 | tf_op jit(solution)/shard_map/ppermute | solution.py:353
  63.7 0.1 convert_add_fusion.1.refs_0_
  63.8 0.1 collective-permute-start.1
  63.9 0.0 collective-permute-done.3.refs_1_
  63.9 13.6 %second_phase.2 = (bf16[24,4096]{1,0:T(8,128)(2,1)S(1)}, f32[24,1536]{1,0:T(8,128)S(1)}, f32[24,1536]{1,0:T(8,128)S(1)}) custom-call(f32[24,12288]{1,0:T(8,128)S(1)} %convert_add_fusion.refs_0_, f32[24,12288]{1,0:T(8,128)S(1)} %collective-permute-done.3.refs_1_, bf16[1536,8192]{1,0:T(8,128)(2,1)} %refs_4_.5, bf16[1536,8192]{1,0:T(8,128)(2,1)} %refs_5_.1, ...), custom_call_target="tpu_custom_call" | custom-call | flops 9663676416 | bytes 37748736 | tf_op jit(solution)/shard_map/second_phase/pallas_call | solution.py:297
  77.5 0.0 collective-permute-done.1.refs_1_
  77.5 14.5 %second_phase.3 = (bf16[24,4096]{1,0:T(8,128)(2,1)S(1)}, bf16[128,768]{1,0:T(8,128)(2,1)}) custom-call(f32[24,12288]{1,0:T(8,128)S(1)} %convert_add_fusion.1.refs_0_, f32[24,12288]{1,0:T(8,128)S(1)} %collective-permute-done.1.refs_1_, f32[24,1536]{1,0:T(8,128)S(1)} %get-tuple-element.25.refs_2_, f32[24,1536]{1,0:T(8,128)S(1)} %get-tuple-element.26.refs_3_, ...), custom_call_target="tpu_custom_call" | custom-call | flops 9663676416 | bytes 37748736 | tf_op jit(solution)/shard_map/second_phase/pallas_call | solution.py:297
  92.0 3.4 %all-to-all-start.1 = ((bf16[8,16,768]{2,1,0:T(8,128)(2,1)}), bf16[8,16,768]{2,1,0:T(8,128)(2,1)S(1)}, u32[]{:S(2)}, u32[]{:S(2)}) async-start(bf16[8,16,768]{2,1,0:T(8,128)(2,1)} %bitcast.2), calls=%async_computation.1 | async-start | bytes 393216 | tf_op jit(solution)/shard_map/all_to_all | solution.py:373
  95.4 10.2 %outer_products.1 = bf16[8192,1536]{1,0:T(8,128)(2,1)} custom-call(bf16[24,4096]{1,0:T(8,128)(2,1)S(1)} %get-tuple-element.31.refs_0_, bf16[24,4096]{1,0:T(8,128)(2,1)S(1)} %get-tuple-element.32.refs_1_, bf16[24,1536]{1,0:T(8,128)(2,1)S(1)} %get-tuple-element.20.refs_1_.refs_2_), custom_call_target="tpu_custom_call" | custom-call | flops 6442450944 | bytes 25165824 | tf_op jit(solution)/shard_map/outer_products/pallas_call | solution.py:335
  105.6 0.0 all-to-all-done.1
  105.6 1.0 combine_rows.1
Async XLA Ops:
  2.1 0.9 copy-start
  3.0 0.8 copy-start.1
  3.9 0.7 copy-start.2
  4.6 0.7 copy-start.3
  5.4 0.7 copy-start.4
  35.8 15.6 %collective-permute-start.2 = (bf16[24,12288]{1,0:T(8,128)(2,1)S(1)}, bf16[24,12288]{1,0:T(8,128)(2,1)S(1)}, u32[]{:S(2)}, u32[]{:S(2)}) collective-permute-start(bf16[24,12288]{1,0:T(8,128)(2,1)S(1)} %get-tuple-element.24), channel_id=1, source_target_pairs={{0,2},{2,0},{1,3},{3,1},{4,6},{6,4},{5,7},{7,5},{8,10},{10,8},{9,1... | collective-permute-start | bytes 1769480 | tf_op jit(solution)/shard_map/ppermute | solution.py:353
  50.8 12.9 %collective-permute-start = (bf16[24,12288]{1,0:T(8,128)(2,1)S(1)}, bf16[24,12288]{1,0:T(8,128)(2,1)S(1)}, u32[]{:S(2)}, u32[]{:S(2)}) collective-permute-start(bf16[24,12288]{1,0:T(8,128)(2,1)S(1)} %get-tuple-element.22), channel_id=1, source_target_pairs={{0,2},{2,0},{1,3},{3,1},{4,6},{6,4},{5,7},{7,5},{8,10},{10,8},{9,1... | collective-permute-start | bytes 1769480 | tf_op jit(solution)/shard_map/ppermute | solution.py:353
  51.5 12.4 %collective-permute-start.3 = (f32[24,12288]{1,0:T(8,128)S(1)}, f32[24,12288]{1,0:T(8,128)S(1)}, u32[]{:S(2)}, u32[]{:S(2)}) collective-permute-start(f32[24,12288]{1,0:T(8,128)S(1)} %convert_add_fusion.refs_0_), channel_id=1, source_target_pairs={{0,16},{16,0},{1,17},{17,1},{2,18},{18,2},{3,19},{19,3},{4,20},{20... | collective-permute-start | bytes 3538952 | tf_op jit(solution)/shard_map/ppermute | solution.py:353
  63.8 13.7 %collective-permute-start.1 = (f32[24,12288]{1,0:T(8,128)S(1)}, f32[24,12288]{1,0:T(8,128)S(1)}, u32[]{:S(2)}, u32[]{:S(2)}) collective-permute-start(f32[24,12288]{1,0:T(8,128)S(1)} %convert_add_fusion.1.refs_0_), channel_id=1, source_target_pairs={{0,16},{16,0},{1,17},{17,1},{2,18},{18,2},{3,19},{19,3},{4,20},{20... | collective-permute-start | bytes 3538952 | tf_op jit(solution)/shard_map/ppermute | solution.py:353
  92.0 13.6 %all-to-all-start.1 = ((bf16[8,16,768]{2,1,0:T(8,128)(2,1)}), bf16[8,16,768]{2,1,0:T(8,128)(2,1)S(1)}, u32[]{:S(2)}, u32[]{:S(2)}) async-start(bf16[8,16,768]{2,1,0:T(8,128)(2,1)} %bitcast.2), calls=%async_computation.1 | async-start | bytes 393216 | tf_op jit(solution)/shard_map/all_to_all | solution.py:373

commit v2 on v1

v2 whole, which is shorter than its diff:
```python
import jax
import jax.numpy as jnp
from jax import lax
from jax.experimental import pallas as pl
from jax.experimental.pallas import tpu as pltpu
from jax.sharding import PartitionSpec as P

EXPERTS = 8
HID = 8192
CAP = 6
KEEP_BLOCKS = 4
SLAB = 16
ROUTE_AXES = ("expert", "tpout")

NN = (((1,), (0,)), ((), ()))
NT = (((1,), (1,)), ((), ()))
TN = (((0,), (0,)), ((), ()))
VMEM = pl.BlockSpec(memory_space=pltpu.VMEM)
ANY = pl.BlockSpec(memory_space=pltpu.HBM)


def dot(left, right, dims=NN, precision=None):
    return lax.dot_general(
        left, right, dims, preferred_element_type=jnp.float32, precision=precision
    )


def params():
    return pltpu.CompilerParams(vmem_limit_bytes=32 << 20)


def cost(flops, nbytes):
    return pl.CostEstimate(flops=int(flops), bytes_accessed=int(nbytes), transcendentals=0)


def route_rows(tokens, cotangent, ids, weights, devices, unit_cols):
    tok_rows, feat = tokens.shape
    rows = devices * SLAB
    top = ids.shape[0]

    def kernel(tok_hbm, cot_hbm, ids_hbm, gw_hbm, send, home, tok, cot, ids_v, gw_v, sems):
        pairs = ((ids_hbm, ids_v), (gw_hbm, gw_v), (tok_hbm, tok), (cot_hbm, cot))
        copies = [
            pltpu.make_async_copy(src, dst, sems.at[i]) for i, (src, dst) in enumerate(pairs)
        ]
        for copy in copies:
            copy.start()
        row = lax.broadcasted_iota(jnp.int32, (rows, tok_rows), 0)
        j = row % SLAB
        want = row // SLAB * unit_cols // HID
        slot = jnp.where(j < 2 * CAP, j % CAP, -1)
        is_x = j < CAP
        earlier = lax.broadcasted_iota(jnp.int32, (tok_rows, tok_rows), 0)
        later = lax.broadcasted_iota(jnp.int32, (tok_rows, tok_rows), 1)
        before = jnp.where(earlier < later, 1.0, 0.0)
        copies[0].wait()
        copies[1].wait()
        hit = jnp.zeros((rows, tok_rows), jnp.float32)
        weight = jnp.zeros((rows, tok_rows), jnp.float32)
        for k in range(top):
            same = ids_v[k : k + 1, :] == want
            hit += jnp.where(same, 1.0, 0.0)
            weight += jnp.where(same, gw_v[k : k + 1, :], 0.0)
        rank = dot(hit, before)
        chosen = jnp.where(rank == slot.astype(jnp.float32), hit, 0.0)
        pick = chosen.astype(jnp.bfloat16)
        row_weight = jnp.sum(chosen * weight, axis=1, keepdims=True)
        home[...] = jnp.where(is_x, chosen * weight, chosen)
        copies[2].wait()
        x = dot(pick, tok[...])
        copies[3].wait()
        dy = row_weight * dot(pick, cot[...])
        send[...] = jnp.where(is_x[:, 0:1], x, dy).astype(jnp.bfloat16)

    return pl.pallas_call(
        kernel,
        in_specs=[ANY] * 4,
        out_specs=[VMEM] * 2,
        out_shape=[
            jax.ShapeDtypeStruct((rows, feat), jnp.bfloat16),
            jax.ShapeDtypeStruct((rows, tok_rows), jnp.float32),
        ],
        scratch_shapes=[
            pltpu.VMEM(tokens.shape, tokens.dtype),
            pltpu.VMEM(cotangent.shape, cotangent.dtype),
            pltpu.VMEM(ids.shape, ids.dtype),
            pltpu.VMEM(weights.shape, weights.dtype),
            pltpu.SemaphoreType.DMA((4,)),
        ],
        compiler_params=pltpu.CompilerParams(vmem_limit_bytes=63 << 20),
        name="route_rows",
    )(tokens, cotangent, ids, weights)


def combine_rows(back, home, tok_rows):
    rows, feat = back.shape

    def kernel(b, h, out, grad):
        j = lax.broadcasted_iota(jnp.int32, h.shape, 0) % SLAB
        vals = b[...].astype(jnp.float32)
        for_out = jnp.where(j < CAP, h[...], 0.0)
        for_grad = jnp.where(j < CAP, 0.0, h[...])
        out[...] = dot(for_out, vals, TN, lax.Precision.HIGHEST).astype(jnp.bfloat16)
        grad[...] = dot(for_grad.astype(jnp.bfloat16), b[...], TN).astype(jnp.bfloat16)

    shape = jax.ShapeDtypeStruct((tok_rows, feat), jnp.bfloat16)
    return pl.pallas_call(
        kernel,
        in_specs=[VMEM] * 2,
        out_specs=[VMEM] * 2,
        out_shape=[shape, shape],
        compiler_params=params(),
        name="combine_rows",
    )(back, home)


class Stream:
    def __init__(self, sources, slots, sems, base, width, steps, kept, present):
        self.sources, self.slots, self.sems = sources, slots, sems
        self.base, self.width, self.steps = base, width, steps
        self.kept, self.present = kept, present
        self.room = kept.shape[1] // width
        self.depth = slots[0].shape[0]

    def place(self, which, step):
        if which == 0 and step < self.room:
            return self.kept.at[:, pl.ds(step * self.width, self.width)]
        return self.slots[which].at[step % self.depth]

    def copy(self, which, step):
        if self.present and which == 0 and step < self.room:
            return None
        at = pl.ds(self.base + step * self.width, self.width)
        source = self.sources[which]
        return pltpu.make_async_copy(
            source.at[at, :] if which == 2 else source.at[:, at],
            self.place(which, step),
            self.sems.at[which, step % self.depth],
        )

    def start(self, which, step):
        copy = self.copy(which, step) if step < self.steps else None
        if copy is not None:
            copy.start()

    def open(self):
        for step in range(self.depth):
            for which in range(3):
                self.start(which, step)

    def take(self, which, step):
        copy = self.copy(which, step)
        if copy is not None:
            copy.wait()
        return self.place(which, step)

    def done(self, which, step):
        self.start(which, step + self.depth)


def stream_scratch(wide, width, depth):
    return [
        pltpu.VMEM((depth, wide, width), jnp.bfloat16),
        pltpu.VMEM((depth, wide, width), jnp.bfloat16),
        pltpu.VMEM((depth, width, wide), jnp.bfloat16),
        pltpu.SemaphoreType.DMA((3, depth)),
    ]


def block_width(cols):
    width = min(512, cols)
    depth = min(4, cols // width)
    return width, depth


def slab_rows(shape, slot_dim, part, outer, counts):
    slot = lax.broadcasted_iota(jnp.int32, shape, slot_dim)
    row = lax.broadcasted_iota(jnp.int32, shape, 1 - slot_dim)
    device = slot // CAP * counts[1] + outer
    place = device * SLAB + part * CAP + slot % CAP
    return jnp.where(row == place, 1.0, 0.0).astype(jnp.bfloat16)


def spread(recv, x_all, dy_all, counts):
    feat = recv.shape[1]
    for outer in range(counts[1]):
        for part, whole in enumerate((x_all, dy_all)):
            pick = slab_rows((whole.shape[0], recv.shape[0]), 0, part, outer, counts)
            whole[:, outer * feat : (outer + 1) * feat] = dot(pick, recv[...]).astype(jnp.bfloat16)


def first_phase(rows_in, w_gate, w_up, w_down, base, cols, counts):
    wide = w_gate.shape[0]
    rows = counts[0] * CAP
    width, depth = block_width(cols)
    steps = cols // width
    keep = min(KEEP_BLOCKS, steps) * width
    opening = len(rows_in) == 1

    def kernel(*refs):
        refs = list(refs)
        rows_refs = [refs.pop(0) for _ in rows_in]
        sources = [refs.pop(0) for _ in range(3)]
        exact, rounded, kept, *refs = refs
        x_all, dy_all = refs[:2] if opening else rows_refs
        *slots, sems = refs[-4:]
        stream = Stream(sources, slots, sems, base, width, steps, kept, False)
        stream.open()
        if opening:
            spread(rows_refs[0], x_all, dy_all, counts)
        for step in range(steps):
            at = step * width
            for i in range(3):
                weight = stream.take(i, step)[...]
                if i < 2:
                    part = dot(x_all[...], weight)
                else:
                    part = dot(dy_all[...], weight, NT)
                here = slice(i * cols + at, i * cols + at + width)
                exact[:, here] = part
                rounded[:, here] = part.astype(jnp.bfloat16)
                stream.done(i, step)

    shapes = [
        jax.ShapeDtypeStruct((rows, 3 * cols), jnp.float32),
        jax.ShapeDtypeStruct((rows, 3 * cols), jnp.bfloat16),
        jax.ShapeDtypeStruct((wide, keep), jnp.bfloat16),
    ]
    if opening:
        shapes += [jax.ShapeDtypeStruct((rows, wide), jnp.bfloat16)] * 2
    return pl.pallas_call(
        kernel,
        in_specs=[VMEM] * len(rows_in) + [ANY] * 3,
        out_specs=[VMEM] * len(shapes),
        out_shape=shapes,
        scratch_shapes=stream_scratch(wide, width, depth),
        compiler_params=params(),
        cost_estimate=cost(6 * 256 * wide * cols, 6 * wide * cols),
        name="first_phase",
    )(*rows_in, w_gate, w_up, w_down)


def second_phase(parts, sums, held, w_gate, w_up, w_down, base, cols, counts, last):
    wide = w_gate.shape[0]
    rows = counts[0] * CAP
    feat = wide // counts[1]
    slabs = counts[0] * counts[1] * SLAB
    width, depth = block_width(cols)
    steps = cols // width

    def kernel(*refs):
        refs = list(refs)
        part_refs = [refs.pop(0) for _ in parts]
        sum_refs = [refs.pop(0) for _ in sums]
        kept = refs.pop(0)
        sources = [refs.pop(0) for _ in range(3)]
        hidden = refs.pop(0)
        outs = [refs.pop(0) for _ in range(1 if last else 2)]
        slots, sems, gate_grad, up_grad = refs[:3], refs[3], refs[4], refs[5]
        acc = refs[6:8] if last else outs
        stream = Stream(sources, slots, sems, base, width, steps, kept, True)
        stream.open()
        for step in range(steps):
            at = step * width
            gate, up, hidden_grad = [
                sum(p[:, i * cols + at : i * cols + at + width].astype(jnp.float32) for p in part_refs)
                for i in range(3)
            ]
            sig = 1.0 / (1.0 + jnp.exp(-gate))
            act = gate * sig
            here = slice(at, at + width)
            hidden[:, here] = (act * up).astype(jnp.bfloat16)
            gate_grad[:, here] = (
                hidden_grad * up * sig * (1.0 + gate * (1.0 - sig))
            ).astype(jnp.bfloat16)
            up_grad[:, here] = (hidden_grad * act).astype(jnp.bfloat16)
        for step in range(steps):
            at = step * width
            here = slice(at, at + width)
            for i, left in enumerate((gate_grad, up_grad, hidden)):
                weight = stream.take(i, step)[...]
                part = dot(left[:, here], weight, NN if i == 2 else NT)
                total = acc[0] if i == 2 else acc[1]
                if step > 0 or i == 1:
                    total[...] += part
                elif sums:
                    total[...] = sum_refs[0 if i == 2 else 1][...] + part
                else:
                    total[...] = part
                stream.done(i, step)
        if last:
            out16 = acc[0][...].astype(jnp.bfloat16)
            grad16 = acc[1][...].astype(jnp.bfloat16)
            packed = []
            for outer in range(counts[1]):
                cut = slice(outer * feat, (outer + 1) * feat)
                picks = [slab_rows((slabs, rows), 1, part, outer, counts) for part in range(2)]
                packed.append(dot(picks[0], out16[:, cut]) + dot(picks[1], grad16[:, cut]))
            outs[0][...] = sum(packed).astype(jnp.bfloat16)

    scratch = stream_scratch(wide, width, depth)
    scratch += [pltpu.VMEM((rows, cols), jnp.bfloat16)] * 2
    shapes = [jax.ShapeDtypeStruct((rows, cols), jnp.bfloat16)]
    if last:
        scratch += [pltpu.VMEM((rows, wide), jnp.float32)] * 2
        shapes += [jax.ShapeDtypeStruct((slabs, feat), jnp.bfloat16)]
    else:
        shapes += [jax.ShapeDtypeStruct((rows, wide), jnp.float32)] * 2
    return pl.pallas_call(
        kernel,
        in_specs=[VMEM] * (len(parts) + len(sums) + 1) + [ANY] * 3,
        out_specs=[VMEM] * len(shapes),
        out_shape=shapes,
        scratch_shapes=scratch,
        compiler_params=params(),
        cost_estimate=cost(6 * 256 * wide * cols, 6 * wide * cols),
        name="second_phase",
    )(*parts, *sums, held, w_gate, w_up, w_down)


def outer_products(hidden, dy_all, chunk, chunks, earlier):
    rows, wide = dy_all.shape
    cols = hidden.shape[1]
    width = min(512, cols)
    total = cols // width
    depth = min(4, total)

    def kernel(*refs):
        hid, dy = refs[:2]
        out, held, sems = refs[-3:]

        def copy(step):
            at = pl.ds(chunk * cols + step * width, width)
            slot = step % depth
            return pltpu.make_async_copy(held.at[slot], out.at[at, :], sems.at[slot])

        for step in range(total):
            if step >= depth:
                copy(step - depth).wait()
            block = hid[:, step * width : (step + 1) * width]
            held[step % depth] = dot(block, dy[...], TN).astype(jnp.bfloat16)
            copy(step).start()
        for step in range(total - depth, total):
            copy(step).wait()

    return pl.pallas_call(
        kernel,
        in_specs=[VMEM] * 2 + [ANY] * len(earlier),
        out_specs=ANY,
        out_shape=jax.ShapeDtypeStruct((cols * chunks, wide), jnp.bfloat16),
        input_output_aliases={2: 0} if earlier else {},
        scratch_shapes=[
            pltpu.VMEM((depth, width, wide), jnp.bfloat16),
            pltpu.SemaphoreType.DMA((depth,)),
        ],
        compiler_params=params(),
        cost_estimate=cost(2 * 256 * wide * cols, 2 * wide * cols),
        name="outer_products",
    )(hidden, dy_all, *earlier)


def from_peers(value, axis):
    size = lax.axis_size(axis)
    return [
        lax.ppermute(value, axis, [(i, (i + hop) % size) for i in range(size)])
        for hop in range(1, size)
    ]


def per_device(tokens, cotangent, expert_ids, gate_weights, w_gate, w_up, w_down):
    expert_count = lax.axis_size("expert")
    outer_count = lax.axis_size("tpout")
    counts = (expert_count, outer_count)
    tok_rows, feat = tokens.shape
    unit_cols = w_gate.shape[1]
    send, home = route_rows(
        tokens, cotangent, expert_ids.T, gate_weights.T, expert_count * outer_count, unit_cols
    )

    def exchange(rows):
        cut = rows.reshape(expert_count * outer_count, SLAB, feat)
        return lax.all_to_all(cut, ROUTE_AXES, 0, 0, tiled=True).reshape(rows.shape)

    rows_in = (exchange(send),)
    chunks = 2 if unit_cols % 1024 == 0 else 1
    cols = unit_cols // chunks
    firsts = []
    for chunk in range(chunks):
        exact, rounded, kept, *opened = first_phase(
            rows_in, w_gate, w_up, w_down, chunk * cols, cols, counts
        )
        if opened:
            rows_in = tuple(opened)
        firsts.append([exact, from_peers(rounded, "tpin"), kept])
        if chunk > 0:
            pair = lax.optimization_barrier((firsts[chunk - 1][0], exact))
            firsts[chunk - 1][0], firsts[chunk][0] = pair
    dy_all = rows_in[1]
    sums, hiddens, down_grad = (), [], ()
    for chunk, (exact, others, kept) in enumerate(firsts):
        if hiddens:
            down_grad = (outer_products(hiddens[-1], dy_all, chunk - 1, chunks, down_grad),)
            exact, sums, down_grad = lax.optimization_barrier((exact, tuple(sums), down_grad))
        mine = exact + sum(o.astype(jnp.float32) for o in others)
        parts = [mine] + from_peers(mine.astype(jnp.bfloat16), "dp")
        last = chunk == chunks - 1
        hidden, *sums = second_phase(
            parts, sums, kept, w_gate, w_up, w_down, chunk * cols, cols, counts, last
        )
        hiddens.append(hidden)
    back = exchange(sums[0])
    down_grad = outer_products(hiddens[-1], dy_all, chunks - 1, chunks, down_grad)
    layer_out, token_grad = combine_rows(back, home, tok_rows)
    return layer_out, token_grad, down_grad


def solution(mesh):
    wide = P("expert", ("dp", "tpin", "tpout"))
    rows = P("expert", None)
    into = P(("dp", "tpin"), ("expert", "tpout"))
    out_of = P(("expert", "tpout"), ("dp", "tpin"))
    return jax.shard_map(
        per_device,
        mesh=mesh,
        in_specs=(wide, wide, rows, rows, into, into, out_of),
        out_specs=(wide, wide, out_of),
        check_vma=False,
    )
```

time: 107 us -> 91.4 us (0.85)
  waiting for transfers between devices: 12.1 us -> 6.04 us
  local copies, waits for them, and re-layouts: 5.42 us -> 0.01 us
  Pallas kernels: 66.6 us -> 62.6 us
    ppermute x4, waiting for transfers between devices: 12.1 us -> 3.21 us  [from_peers(): lax.ppermute(value, axis, [(i, (i + hop) % size) for i in range(size)])]
    unnamed x12 -> x2, local copies, waits for them, and re-layouts: 5.42 us -> 0.01 us
    pallas_call x4 -> x5, Pallas kernels: 38.8 us -> 35.8 us  [the longest x2 23 us: second_phase(): pl.pallas_call(kernel, in_specs=[VMEM] * (len(parts) + len(sums) + 1) + [...]
    all_to_all x1, waiting for transfers between devices: 0.01 us -> 2.83 us  [exchange(): return lax.all_to_all(cut, ROUTE_AXES, 0, 0, tiled=True).reshape(rows.shape)]
    pallas_call x2, Pallas kernels: 26.9 us -> 25.8 us  [first_phase(): pl.pallas_call(kernel, in_specs=[VMEM] * len(rows_in) + [ANY] * 3, out_sp...]
  transfers between devices with their start and end apart: 5 -> 5, of which waited for: 1 -> 3; matrix products, arithmetic and copies ran while one was open for 0% -> 0% of each run, Pallas kernels for 35% -> 38%
where the time goes in v2:
time: 91.4 us; the launch traced here: 91 us
  Pallas kernels  62.6 us (68%)
  blocking collectives  15.2 us (17%)
  starting transfers between devices  6.13 us (7%)
  waiting for transfers between devices  6.04 us (7%)
    pallas_call x2, Pallas kernels, first_phase(): pl.pallas_call(kernel, in_specs=[VMEM] * len(rows_in) + [ANY] * 3, out_sp...  25.8 us
    pallas_call x2, Pallas kernels, second_phase(): pl.pallas_call(kernel, in_specs=[VMEM] * (len(parts) + len(sums) + 1) + [...  23 us
    all_to_all x1, blocking collectives, exchange(): return lax.all_to_all(cut, ROUTE_AXES, 0, 0, tiled=True).reshape(rows.shape)  15.2 us
    pallas_call x2, Pallas kernels, outer_products(): pl.pallas_call(kernel, in_specs=[VMEM] * 2 + [ANY] * len(earlier), out_sp...  10.8 us
    all_to_all x1, starting transfers between devices, exchange(): return lax.all_to_all(cut, ROUTE_AXES, 0, 0, tiled=True).reshape(rows.shape)  3.62 us
    ppermute x4, waiting for transfers between devices, from_peers(): lax.ppermute(value, axis, [(i, (i + hop) % size) for i in range(size)])  3.21 us
    all_to_all x1, waiting for transfers between devices, exchange(): return lax.all_to_all(cut, ROUTE_AXES, 0, 0, tiled=True).reshape(rows.shape)  2.83 us
    ppermute x4, starting transfers between devices, from_peers(): lax.ppermute(value, axis, [(i, (i + hop) % size) for i in range(size)])  2.51 us
  transfers between devices with their start and end apart: 5, of which 3 were waited for; matrix products, arithmetic and copies ran while one was open for 0% of the time, Pallas kernels for 38%

profile of v2, /device:TPU:0, one launch (start us, length us, event | category | flops | bytes accessed | tf_op | source)
XLA Modules:
  0.0 91.0 jit_solution(8231042826922595050)
XLA Ops:
  0.6 2.0 %route_rows.1 = (bf16[128,768]{1,0:T(8,128)(2,1)}, f32[128,16]{1,0:T(8,128)}) custom-call(bf16[16,768]{1,0:T(8,128)(2,1)} %tok_hbm.1, bf16[16,768]{1,0:T(8,128)(2,1)} %cot_hbm.1, s32[2,16]{1,0:T(2,128)} %bitcast.9, f32[2,16]{1,0:T(2,128)} %bitcast.10), custom_call_target="tpu_custom_call" | custom-call | tf_op jit(solution)/shard_map/route_rows/pallas_call | solution.py:75
  2.6 15.2 %all_to_all.10 = bf16[8,16,768]{2,1,0:T(8,128)(2,1)S(1)} all-to-all(bf16[8,16,768]{2,1,0:T(8,128)(2,1)} %bitcast.8), channel_id=1, replica_groups=mesh['dp'=2,'expert'=4,'tpin'=2,'tpout'=2] {'expert','tpout'}, dimensions={0} | all-to-all | bytes 393216 | tf_op jit(solution)/shard_map/all_to_all | solution.py:382
  17.9 12.9 %first_phase.2 = (f32[24,12288]{1,0:T(8,128)S(1)}, bf16[24,12288]{1,0:T(8,128)(2,1)S(1)}, bf16[1536,2048]{1,0:T(8,128)(2,1)S(1)}, bf16[24,1536]{1,0:T(8,128)(2,1)S(1)}, bf16[24,1536]{1,0:T(8,128)(2,1)S(1)}) custom-call(bf16[128,768]{1,0:T(8,128)(2,1)S(1)} %bitcast.7, bf16[1536,8192]{1,0:T(8,128)(2,1)} %refs_5_.3, bf16[1536,8192]{1,0:T(8,128)(2,1)} %refs_6_.1, ...), custom_call_target="tpu_custom_call" | custom-call | flops 9663676416 | bytes 37748736 | tf_op jit(solution)/shard_map/first_phase/pallas_call | solution.py:231
  30.8 1.6 %collective-permute-start = (bf16[24,12288]{1,0:T(8,128)(2,1)S(1)}, bf16[24,12288]{1,0:T(8,128)(2,1)S(1)}, u32[]{:S(2)}, u32[]{:S(2)}) collective-permute-start(bf16[24,12288]{1,0:T(8,128)(2,1)S(1)} %get-tuple-element.33), channel_id=1, source_target_pairs={{0,2},{2,0},{1,3},{3,1},{4,6},{6,4},{5,7},{7,5},{8,10},{10,8},{9,1... | collective-permute-start | bytes 1769480 | tf_op jit(solution)/shard_map/ppermute | solution.py:365
  32.4 12.9 %first_phase.3 = (f32[24,12288]{1,0:T(8,128)S(1)}, bf16[24,12288]{1,0:T(8,128)(2,1)S(1)}, bf16[1536,2048]{1,0:T(8,128)(2,1)S(1)}) custom-call(bf16[24,1536]{1,0:T(8,128)(2,1)S(1)} %get-tuple-element.28.refs_0_, bf16[24,1536]{1,0:T(8,128)(2,1)S(1)} %get-tuple-element.29.refs_1_, bf16[1536,8192]{1,0:T(8,128)(2,1)} %refs_5_.3, bf16[1536,8192]{1,0:T(8,128)(2,1)} %refs_6_.1, ...), custom_call_target="tpu_custom_call" | custom-call | flops 9663676416 | bytes 37748736 | tf_op jit(solution)/shard_map/first_phase/pallas_call | solution.py:231
  45.3 0.0 collective-permute-done
  45.3 0.1 fusion.1
  45.4 0.1 collective-permute-start.1
  45.5 0.7 collective-permute-start.2
  46.1 1.3 %collective-permute-done.1.refs_1_ = bf16[24,12288]{1,0:T(8,128)(2,1)S(1)} collective-permute-done((bf16[24,12288]{1,0:T(8,128)(2,1)S(1)}, bf16[24,12288]{1,0:T(8,128)(2,1)S(1)}, u32[]{:S(2)}, u32[]{:S(2)}) %collective-permute-start.1) | collective-permute-done | bytes 589856 | tf_op jit(solution)/shard_map/ppermute | solution.py:365
  47.5 11.1 %second_phase.2 = (bf16[24,4096]{1,0:T(8,128)(2,1)S(1)}, f32[24,1536]{1,0:T(8,128)S(1)}, f32[24,1536]{1,0:T(8,128)S(1)}) custom-call(f32[24,12288]{1,0:T(8,128)S(1)} %get-tuple-element.52.refs_0_, bf16[24,12288]{1,0:T(8,128)(2,1)S(1)} %collective-permute-done.1.refs_1_, bf16[1536,2048]{1,0:T(8,128)(2,1)S(1)} %get-tuple-element.34.refs_2_, ...), custom_call_target="tpu_custom_call" | custom-call | flops 9663676416 | bytes 37748736 | tf_op jit(solution)/shard_map/second_phase/pallas_call | solution.py:309
  58.5 5.4 %outer_products.2.refs_2_ = bf16[8192,1536]{1,0:T(8,128)(2,1)} custom-call(bf16[24,4096]{1,0:T(8,128)(2,1)S(1)} %get-tuple-element.37.refs_0_, bf16[24,1536]{1,0:T(8,128)(2,1)S(1)} %get-tuple-element.29.refs_1_), custom_call_target="tpu_custom_call" | custom-call | flops 3221225472 | bytes 12582912 | tf_op jit(solution)/shard_map/outer_products/pallas_call | solution.py:346
  63.9 0.0 collective-permute-done.2
  63.9 0.1 fusion
  64.1 0.2 collective-permute-start.3
  64.3 1.9 %collective-permute-done.3.refs_1_ = bf16[24,12288]{1,0:T(8,128)(2,1)S(1)} collective-permute-done((bf16[24,12288]{1,0:T(8,128)(2,1)S(1)}, bf16[24,12288]{1,0:T(8,128)(2,1)S(1)}, u32[]{:S(2)}, u32[]{:S(2)}) %collective-permute-start.3) | collective-permute-done | bytes 589856 | tf_op jit(solution)/shard_map/ppermute | solution.py:365
  66.1 12.0 %second_phase.3 = (bf16[24,4096]{1,0:T(8,128)(2,1)S(1)}, bf16[128,768]{1,0:T(8,128)(2,1)}) custom-call(f32[24,12288]{1,0:T(8,128)S(1)} %get-tuple-element.50.refs_0_, bf16[24,12288]{1,0:T(8,128)(2,1)S(1)} %collective-permute-done.3.refs_1_, f32[24,1536]{1,0:T(8,128)S(1)} %get-tuple-element.40.refs_2_, f32[24,1536]{1,0:T(8,128)S(1)} %get-tuple-element.41.refs_3_, ...), custom_call_target="tpu_custom_call" | custom-call | flops 9663676416 | bytes 37748736 | tf_op jit(solution)/shard_map/second_phase/pallas_call | solution.py:309
  78.1 3.6 %all-to-all-start.1 = ((bf16[8,16,768]{2,1,0:T(8,128)(2,1)}), bf16[8,16,768]{2,1,0:T(8,128)(2,1)S(1)}, u32[]{:S(2)}, u32[]{:S(2)}) async-start(bf16[8,16,768]{2,1,0:T(8,128)(2,1)} %bitcast.4), calls=%async_computation.1 | async-start | bytes 393216 | tf_op jit(solution)/shard_map/all_to_all | solution.py:382
  81.8 0.0 copy-start
  81.8 5.4 %outer_products.3 = bf16[8192,1536]{1,0:T(8,128)(2,1)} custom-call(bf16[24,4096]{1,0:T(8,128)(2,1)S(1)} %get-tuple-element.47.refs_0_, bf16[24,1536]{1,0:T(8,128)(2,1)S(1)} %get-tuple-element.29.refs_1_, bf16[8192,1536]{1,0:T(8,128)(2,1)} %outer_products.2.refs_2_), custom_call_target="tpu_custom_call", output_to_operand_aliasing={{}: (2, {})} | custom-call | flops 3221225472 | bytes 12582912 | tf_op jit(solution)/shard_map/outer_products/pallas_call | solution.py:346
  87.2 2.8 %all-to-all-done.1 = bf16[8,16,768]{2,1,0:T(8,128)(2,1)S(1)} async-done(((bf16[8,16,768]{2,1,0:T(8,128)(2,1)}), bf16[8,16,768]{2,1,0:T(8,128)(2,1)S(1)}, u32[]{:S(2)}, u32[]{:S(2)}) %all-to-all-start.1) | async-done | bytes 196640 | tf_op jit(solution)/shard_map/all_to_all | solution.py:382
  90.0 0.0 copy-done
  90.0 1.0 %combine_rows.1 = (bf16[16,768]{1,0:T(8,128)(2,1)}, bf16[16,768]{1,0:T(8,128)(2,1)}) custom-call(bf16[128,768]{1,0:T(8,128)(2,1)S(1)} %bitcast.6, f32[128,16]{1,0:T(8,128)S(1)} %copy-done), custom_call_target="tpu_custom_call" | custom-call | tf_op jit(solution)/shard_map/combine_rows/pallas_call | solution.py:107
Async XLA Ops:
  30.8 14.5 %collective-permute-start = (bf16[24,12288]{1,0:T(8,128)(2,1)S(1)}, bf16[24,12288]{1,0:T(8,128)(2,1)S(1)}, u32[]{:S(2)}, u32[]{:S(2)}) collective-permute-start(bf16[24,12288]{1,0:T(8,128)(2,1)S(1)} %get-tuple-element.33), channel_id=1, source_target_pairs={{0,2},{2,0},{1,3},{3,1},{4,6},{6,4},{5,7},{7,5},{8,10},{10,8},{9,1... | collective-permute-start | bytes 1769480 | tf_op jit(solution)/shard_map/ppermute | solution.py:365
  45.4 2.1 %collective-permute-start.1 = (bf16[24,12288]{1,0:T(8,128)(2,1)S(1)}, bf16[24,12288]{1,0:T(8,128)(2,1)S(1)}, u32[]{:S(2)}, u32[]{:S(2)}) collective-permute-start(bf16[24,12288]{1,0:T(8,128)(2,1)S(1)} %get-tuple-element.51), channel_id=1, source_target_pairs={{0,16},{16,0},{1,17},{17,1},{2,18},{18,2},{3,19},{19,3},{4,20},{20... | collective-permute-start | bytes 1769480 | tf_op jit(solution)/shard_map/ppermute | solution.py:365
  45.5 18.5 %collective-permute-start.2 = (bf16[24,12288]{1,0:T(8,128)(2,1)S(1)}, bf16[24,12288]{1,0:T(8,128)(2,1)S(1)}, u32[]{:S(2)}, u32[]{:S(2)}) collective-permute-start(bf16[24,12288]{1,0:T(8,128)(2,1)S(1)} %get-tuple-element.39), channel_id=1, source_target_pairs={{0,2},{2,0},{1,3},{3,1},{4,6},{6,4},{5,7},{7,5},{8,10},{10,8},{9,1... | collective-permute-start | bytes 1769480 | tf_op jit(solution)/shard_map/ppermute | solution.py:365
  64.1 2.1 %collective-permute-start.3 = (bf16[24,12288]{1,0:T(8,128)(2,1)S(1)}, bf16[24,12288]{1,0:T(8,128)(2,1)S(1)}, u32[]{:S(2)}, u32[]{:S(2)}) collective-permute-start(bf16[24,12288]{1,0:T(8,128)(2,1)S(1)} %get-tuple-element.49), channel_id=1, source_target_pairs={{0,16},{16,0},{1,17},{17,1},{2,18},{18,2},{3,19},{19,3},{4,20},{20... | collective-permute-start | bytes 1769480 | tf_op jit(solution)/shard_map/ppermute | solution.py:365
  78.1 11.9 %all-to-all-start.1 = ((bf16[8,16,768]{2,1,0:T(8,128)(2,1)}), bf16[8,16,768]{2,1,0:T(8,128)(2,1)S(1)}, u32[]{:S(2)}, u32[]{:S(2)}) async-start(bf16[8,16,768]{2,1,0:T(8,128)(2,1)} %bitcast.4), calls=%async_computation.1 | async-start | bytes 393216 | tf_op jit(solution)/shard_map/all_to_all | solution.py:382
  81.8 8.3 %copy-start = (f32[128,16]{1,0:T(8,128)S(1)}, f32[128,16]{1,0:T(8,128)}, u32[]{:S(2)}) copy-start(f32[128,16]{1,0:T(8,128)} %get-tuple-element.44.h) | copy-start | bytes 24580

commit v3 on v2

v3 whole, which is shorter than its diff:
```python
import jax
import jax.numpy as jnp
from jax import lax
from jax.experimental import pallas as pl
from jax.experimental.pallas import tpu as pltpu
from jax.sharding import PartitionSpec as P

EXPERTS = 8
HID = 8192
CAP = 6
BLOCK = 512
DEPTH = 4
KEEP_BLOCKS = 4
FIRST_SHARE = 16
EARLY_BLOCKS = 3
SLAB = 16
ROUTE_AXES = ("expert", "tpout")

NN = (((1,), (0,)), ((), ()))
NT = (((1,), (1,)), ((), ()))
TN = (((0,), (0,)), ((), ()))
VMEM = pl.BlockSpec(memory_space=pltpu.VMEM)
ANY = pl.BlockSpec(memory_space=pltpu.HBM)


def dot(left, right, dims=NN, precision=None):
    return lax.dot_general(
        left, right, dims, preferred_element_type=jnp.float32, precision=precision
    )


def params(mib=16):
    return pltpu.CompilerParams(vmem_limit_bytes=mib << 20)


def cost(flops, nbytes):
    return pl.CostEstimate(flops=int(flops), bytes_accessed=int(nbytes), transcendentals=0)


def route_rows(tokens, cotangent, ids, weights, devices, unit_cols):
    tok_rows, feat = tokens.shape
    rows = devices * SLAB
    top = ids.shape[0]

    def kernel(tok_hbm, cot_hbm, ids_hbm, gw_hbm, send, home, tok, cot, ids_v, gw_v, sems):
        pairs = ((ids_hbm, ids_v), (gw_hbm, gw_v), (tok_hbm, tok), (cot_hbm, cot))
        copies = [
            pltpu.make_async_copy(src, dst, sems.at[i]) for i, (src, dst) in enumerate(pairs)
        ]
        for copy in copies:
            copy.start()
        row = lax.broadcasted_iota(jnp.int32, (rows, tok_rows), 0)
        j = row % SLAB
        want = row // SLAB * unit_cols // HID
        slot = jnp.where(j < 2 * CAP, j % CAP, -1)
        is_x = j < CAP
        earlier = lax.broadcasted_iota(jnp.int32, (tok_rows, tok_rows), 0)
        later = lax.broadcasted_iota(jnp.int32, (tok_rows, tok_rows), 1)
        before = jnp.where(earlier < later, 1.0, 0.0)
        copies[0].wait()
        copies[1].wait()
        hit = jnp.zeros((rows, tok_rows), jnp.float32)
        weight = jnp.zeros((rows, tok_rows), jnp.float32)
        for k in range(top):
            same = ids_v[k : k + 1, :] == want
            hit += jnp.where(same, 1.0, 0.0)
            weight += jnp.where(same, gw_v[k : k + 1, :], 0.0)
        rank = dot(hit, before)
        chosen = jnp.where(rank == slot.astype(jnp.float32), hit, 0.0)
        pick = chosen.astype(jnp.bfloat16)
        row_weight = jnp.sum(chosen * weight, axis=1, keepdims=True)
        home[...] = jnp.where(is_x, chosen * weight, chosen)
        copies[2].wait()
        x = dot(pick, tok[...])
        copies[3].wait()
        dy = row_weight * dot(pick, cot[...])
        send[...] = jnp.where(is_x[:, 0:1], x, dy).astype(jnp.bfloat16)

    return pl.pallas_call(
        kernel,
        in_specs=[ANY] * 4,
        out_specs=[VMEM] * 2,
        out_shape=[
            jax.ShapeDtypeStruct((rows, feat), jnp.bfloat16),
            jax.ShapeDtypeStruct((rows, tok_rows), jnp.float32),
        ],
        scratch_shapes=[
            pltpu.VMEM(tokens.shape, tokens.dtype),
            pltpu.VMEM(cotangent.shape, cotangent.dtype),
            pltpu.VMEM(ids.shape, ids.dtype),
            pltpu.VMEM(weights.shape, weights.dtype),
            pltpu.SemaphoreType.DMA((4,)),
        ],
        compiler_params=params(63),
        name="route_rows",
    )(tokens, cotangent, ids, weights)


def combine_rows(back, home, tok_rows):
    rows, feat = back.shape

    def kernel(b, h, out, grad):
        j = lax.broadcasted_iota(jnp.int32, h.shape, 0) % SLAB
        vals = b[...].astype(jnp.float32)
        for_out = jnp.where(j < CAP, h[...], 0.0)
        for_grad = jnp.where(j < CAP, 0.0, h[...])
        out[...] = dot(for_out, vals, TN, lax.Precision.HIGHEST).astype(jnp.bfloat16)
        grad[...] = dot(for_grad.astype(jnp.bfloat16), b[...], TN).astype(jnp.bfloat16)

    shape = jax.ShapeDtypeStruct((tok_rows, feat), jnp.bfloat16)
    return pl.pallas_call(
        kernel,
        in_specs=[VMEM] * 2,
        out_specs=[VMEM] * 2,
        out_shape=[shape, shape],
        compiler_params=params(),
        name="combine_rows",
    )(back, home)


def block_list(cols):
    return [(at, min(BLOCK, cols - at)) for at in range(0, cols, BLOCK)]


class Stream:
    def __init__(self, sources, slots, sems, base, blocks, stays):
        self.sources, self.slots, self.sems = sources, slots, sems
        self.base, self.blocks, self.stays = base, blocks, stays

    def place(self, which, step):
        at, width = self.blocks[step]
        ref, count, offset, _ = self.stays.get(which, (None, 0, 0, False))
        if step < count:
            return ref.at[:, pl.ds(offset + at, width)]
        slot = self.slots[which].at[step % DEPTH]
        if width == BLOCK:
            return slot
        return slot.at[pl.ds(0, width), :] if which == 2 else slot.at[:, pl.ds(0, width)]

    def copy(self, which, step):
        _, count, _, present = self.stays.get(which, (None, 0, 0, False))
        if present and step < count:
            return None
        at, width = self.blocks[step]
        at = pl.ds(self.base + at, width)
        source = self.sources[which]
        return pltpu.make_async_copy(
            source.at[at, :] if which == 2 else source.at[:, at],
            self.place(which, step),
            self.sems.at[which, step % DEPTH],
        )

    def start(self, which, step):
        copy = self.copy(which, step) if step < len(self.blocks) else None
        if copy is not None:
            copy.start()

    def open(self):
        for step in range(DEPTH):
            for which in range(3):
                self.start(which, step)

    def take(self, which, step):
        copy = self.copy(which, step)
        if copy is not None:
            copy.wait()
        return self.place(which, step)

    def done(self, which, step):
        self.start(which, step + DEPTH)


def stream_scratch(wide, weights):
    slots = [
        pltpu.VMEM((DEPTH, BLOCK, wide) if which == 2 else (DEPTH, wide, BLOCK), jnp.bfloat16)
        for which in weights
    ]
    return slots + [pltpu.SemaphoreType.DMA((3, DEPTH))]


def slab_rows(shape, slot_dim, part, outer, counts):
    slot = lax.broadcasted_iota(jnp.int32, shape, slot_dim)
    row = lax.broadcasted_iota(jnp.int32, shape, 1 - slot_dim)
    device = slot // CAP * counts[1] + outer
    place = device * SLAB + part * CAP + slot % CAP
    return jnp.where(row == place, 1.0, 0.0).astype(jnp.bfloat16)


def spread(recv, x_all, dy_all, counts):
    feat = recv.shape[1]
    for outer in range(counts[1]):
        for part, whole in enumerate((x_all, dy_all)):
            pick = slab_rows((whole.shape[0], recv.shape[0]), 0, part, outer, counts)
            whole[:, outer * feat : (outer + 1) * feat] = dot(pick, recv[...]).astype(jnp.bfloat16)


def streamed(held, blocks):
    return [i for i in range(3) if i not in held or held[i][2] < len(blocks)]


def first_phase(rows_in, weights, held, saves, base, cols, counts):
    wide = weights[0].shape[0]
    rows = counts[0] * CAP
    blocks = block_list(cols)
    opening = len(rows_in) == 1
    live = streamed(held, blocks)
    sources_at = sorted(set(live) | {save[0] for save in saves})

    def kernel(*refs):
        refs = list(refs)
        rows_refs = [refs.pop(0) for _ in rows_in]
        stays = {i: (refs.pop(0), held[i][2], held[i][1], True) for i in held}
        sources = {i: refs.pop(0) for i in sources_at}
        exact, rounded = refs.pop(0), refs.pop(0)
        for i, _, units in saves:
            stays[i] = (refs.pop(0), len(block_list(units)), 0, False)
        x_all, dy_all = (refs.pop(0), refs.pop(0)) if opening else rows_refs
        slots = {i: refs.pop(0) for i in live}
        sems = refs.pop(0)
        stream = Stream(sources, slots, sems, base, blocks, stays)
        stream.open()
        if opening:
            spread(rows_refs[0], x_all, dy_all, counts)
        for step, (at, width) in enumerate(blocks):
            for i in range(3):
                weight = stream.take(i, step)[...]
                if i < 2:
                    part = dot(x_all[...], weight)
                else:
                    part = dot(dy_all[...], weight, NT)
                here = slice(i * cols + at, i * cols + at + width)
                exact[:, here] = part
                rounded[:, here] = part.astype(jnp.bfloat16)
                stream.done(i, step)

    shapes = [
        jax.ShapeDtypeStruct((rows, 3 * cols), jnp.float32),
        jax.ShapeDtypeStruct((rows, 3 * cols), jnp.bfloat16),
    ]
    shapes += [jax.ShapeDtypeStruct((wide, units), jnp.bfloat16) for _, _, units in saves]
    if opening:
        shapes += [jax.ShapeDtypeStruct((rows, wide), jnp.bfloat16)] * 2
    scratch = stream_scratch(wide, live)
    return pl.pallas_call(
        kernel,
        in_specs=[VMEM] * (len(rows_in) + len(held)) + [ANY] * len(sources_at),
        out_specs=[VMEM] * len(shapes),
        out_shape=shapes,
        scratch_shapes=scratch,
        compiler_params=params(6 * len(live) + 8),
        cost_estimate=cost(6 * 256 * wide * cols, 6 * wide * cols),
        name="first_phase",
    )(*rows_in, *[held[i][0] for i in held], *[weights[i] for i in sources_at])


def second_phase(parts, sums, weights, held, base, cols, counts, last):
    wide = weights[0].shape[0]
    rows = counts[0] * CAP
    feat = wide // counts[1]
    slabs = counts[0] * counts[1] * SLAB
    blocks = block_list(cols)
    live = streamed(held, blocks)
    order = (1, 0, 2) if 1 in held else (0, 1, 2)

    def kernel(*refs):
        refs = list(refs)
        part_refs = [refs.pop(0) for _ in parts]
        sum_refs = [refs.pop(0) for _ in sums]
        stays = {i: (refs.pop(0), held[i][2], held[i][1], True) for i in held}
        sources = {i: refs.pop(0) for i in live}
        hidden = refs.pop(0)
        outs = [refs.pop(0) for _ in range(1 if last else 2)]
        slots = {i: refs.pop(0) for i in live}
        sems, gate_grad, up_grad, *rest = refs
        acc = rest[:2] if last else outs
        stream = Stream(sources, slots, sems, base, blocks, stays)
        stream.open()
        for at, width in blocks:
            gate, up, hidden_grad = [
                sum(p[:, i * cols + at : i * cols + at + width].astype(jnp.float32) for p in part_refs)
                for i in range(3)
            ]
            sig = 1.0 / (1.0 + jnp.exp(-gate))
            act = gate * sig
            here = slice(at, at + width)
            hidden[:, here] = (act * up).astype(jnp.bfloat16)
            gate_grad[:, here] = (
                hidden_grad * up * sig * (1.0 + gate * (1.0 - sig))
            ).astype(jnp.bfloat16)
            up_grad[:, here] = (hidden_grad * act).astype(jnp.bfloat16)
        if last:
            packed = rest[2]
            packed[...] = jnp.zeros_like(packed)
        filled = [False, False]
        for step, (at, width) in enumerate(blocks):
            here = slice(at, at + width)
            for i in order:
                weight = stream.take(i, step)[...]
                left = (gate_grad, up_grad, hidden)[i]
                part = dot(left[:, here], weight, NN if i == 2 else NT)
                which = 0 if i == 2 else 1
                if filled[which]:
                    acc[which][...] += part
                elif sums:
                    acc[which][...] = sum_refs[which][...] + part
                else:
                    acc[which][...] = part
                filled[which] = True
                stream.done(i, step)
        if last:
            for device in range(counts[0] * counts[1]):
                block, outer = device // counts[1], device % counts[1]
                for which in range(2):
                    to = device * SLAB + which * CAP
                    packed[to : to + CAP, :] = acc[which][
                        block * CAP : (block + 1) * CAP, outer * feat : (outer + 1) * feat
                    ]
            outs[0][...] = packed[...].astype(jnp.bfloat16)

    scratch = stream_scratch(wide, live)
    scratch += [pltpu.VMEM((rows, cols), jnp.bfloat16)] * 2
    shapes = [jax.ShapeDtypeStruct((rows, cols), jnp.bfloat16)]
    if last:
        scratch += [pltpu.VMEM((rows, wide), jnp.float32)] * 2
        scratch += [pltpu.VMEM((slabs, feat), jnp.float32)]
        shapes += [jax.ShapeDtypeStruct((slabs, feat), jnp.bfloat16)]
    else:
        shapes += [jax.ShapeDtypeStruct((rows, wide), jnp.float32)] * 2
    return pl.pallas_call(
        kernel,
        in_specs=[VMEM] * (len(parts) + len(sums) + len(held)) + [ANY] * len(live),
        out_specs=[VMEM] * len(shapes),
        out_shape=shapes,
        scratch_shapes=scratch,
        compiler_params=params(6 * len(live) + 10),
        cost_estimate=cost(6 * 256 * wide * cols, 6 * wide * cols),
        name="second_phase",
    )(*parts, *sums, *[held[i][0] for i in held], *[weights[i] for i in live])


def outer_products(hiddens, dy_all, blocks, shape, earlier):
    wide = shape[1]

    def kernel(*refs):
        hidden_refs, dy = refs[: len(hiddens)], refs[len(hiddens)]
        out, held, sems = refs[-3:]

        def copy(i):
            _, _, row, width = blocks[i]
            slot = held.at[i % DEPTH]
            source = slot if width == BLOCK else slot.at[pl.ds(0, width), :]
            return pltpu.make_async_copy(source, out.at[pl.ds(row, width), :], sems.at[i % DEPTH])

        for i, (chunk, at, _, width) in enumerate(blocks):
            if i >= DEPTH:
                copy(i - DEPTH).wait()
            left = hidden_refs[chunk][:, at : at + width]
            held[i % DEPTH, 0:width, :] = dot(left, dy[...], TN).astype(jnp.bfloat16)
            copy(i).start()
        for i in range(max(0, len(blocks) - DEPTH), len(blocks)):
            copy(i).wait()

    total = sum(block[3] for block in blocks)
    return pl.pallas_call(
        kernel,
        in_specs=[VMEM] * (len(hiddens) + 1) + [ANY] * len(earlier),
        out_specs=ANY,
        out_shape=jax.ShapeDtypeStruct(shape, jnp.bfloat16),
        input_output_aliases={len(hiddens) + 1: 0} if earlier else {},
        scratch_shapes=[
            pltpu.VMEM((DEPTH, BLOCK, wide), jnp.bfloat16),
            pltpu.SemaphoreType.DMA((DEPTH,)),
        ],
        compiler_params=params(),
        cost_estimate=cost(2 * 256 * wide * total, 2 * wide * total),
        name="outer_products",
    )(*hiddens, dy_all, *earlier)


def from_peers(value, axis):
    size = lax.axis_size(axis)
    return [
        lax.ppermute(value, axis, [(i, (i + hop) % size) for i in range(size)])
        for hop in range(1, size)
    ]


def per_device(tokens, cotangent, expert_ids, gate_weights, w_gate, w_up, w_down):
    expert_count = lax.axis_size("expert")
    outer_count = lax.axis_size("tpout")
    counts = (expert_count, outer_count)
    tok_rows, feat = tokens.shape
    unit_cols = w_gate.shape[1]
    send, home = route_rows(
        tokens, cotangent, expert_ids.T, gate_weights.T, expert_count * outer_count, unit_cols
    )

    def exchange(rows):
        cut = rows.reshape(expert_count * outer_count, SLAB, feat)
        return lax.all_to_all(cut, ROUTE_AXES, 0, 0, tiled=True).reshape(rows.shape)

    weights = (w_gate, w_up, w_down)
    first_cols = unit_cols * FIRST_SHARE // 32 // 256 * 256 if unit_cols >= 4 * BLOCK else 0
    chunks = [(0, first_cols)] if first_cols else []
    chunks += [(first_cols, unit_cols - first_cols)]
    keeps = [min(KEEP_BLOCKS * BLOCK, cols // BLOCK * BLOCK or cols) for _, cols in chunks]
    rows_in = (exchange(send),)
    firsts, saved = [], []
    for n, (base, cols) in enumerate(chunks):
        saves = [(0, base, keeps[n])]
        exact, rounded, *more = first_phase(
            rows_in, weights, {}, saves, base, cols, counts
        )
        for i, _, units in saves:
            saved.append({i: (more.pop(0), 0, len(block_list(units)))})
        if more:
            rows_in = tuple(more)
        if firsts:
            before, exact = lax.optimization_barrier((firsts[-1][0], exact))
            firsts[-1][0] = before
        firsts.append([exact, from_peers(rounded, "tpin")])
    dy_all = rows_in[1]
    blocks = [
        (i, at, base + at, width)
        for i, (base, cols) in enumerate(chunks)
        for at, width in block_list(cols)
    ]
    sums, hiddens, down_grad = (), [], ()
    for (base, cols), (exact, others), held in zip(chunks, firsts, saved):
        last = base + cols == unit_cols
        if hiddens:
            early, blocks = blocks[:EARLY_BLOCKS], blocks[EARLY_BLOCKS:]
            down_grad = (outer_products(hiddens, dy_all, early, w_down.shape, down_grad),)
            exact, sums, down_grad = lax.optimization_barrier((exact, tuple(sums), down_grad))
        mine = exact + sum(o.astype(jnp.float32) for o in others)
        parts = [mine] + from_peers(mine.astype(jnp.bfloat16), "dp")
        hidden, *sums = second_phase(
            parts, sums, weights, held, base, cols, counts, last
        )
        hiddens.append(hidden)
    back = exchange(sums[0])
    down_grad = outer_products(hiddens, dy_all, blocks, w_down.shape, down_grad)
    layer_out, token_grad = combine_rows(back, home, tok_rows)
    return layer_out, token_grad, down_grad


def solution(mesh):
    wide = P("expert", ("dp", "tpin", "tpout"))
    rows = P("expert", None)
    into = P(("dp", "tpin"), ("expert", "tpout"))
    out_of = P(("expert", "tpout"), ("dp", "tpin"))
    return jax.shard_map(
        per_device,
        mesh=mesh,
        in_specs=(wide, wide, rows, rows, into, into, out_of),
        out_specs=(wide, wide, out_of),
        check_vma=False,
    )
```

time: 91.4 us -> 88.7 us (0.970)
  waiting for transfers between devices: 6.04 us -> 3.21 us
    all_to_all x1, waiting for transfers between devices: 2.83 us -> 0.01 us  [exchange(): return lax.all_to_all(cut, ROUTE_AXES, 0, 0, tiled=True).reshape(rows.shape)]
  transfers between devices with their start and end apart: 5 -> 5, of which waited for: 3 -> 2; matrix products, arithmetic and copies ran while one was open for 0% -> 0% of each run, Pallas kernels for 38% -> 40%
where the time goes in v3:
time: 88.7 us; the launch traced here: 88.3 us
  Pallas kernels  62.8 us (71%)
  blocking collectives  15.2 us (17%)
  starting transfers between devices  6.13 us (7%)
  waiting for transfers between devices  3.21 us (4%)
    pallas_call x2, Pallas kernels, first_phase(): pl.pallas_call(kernel, in_specs=[VMEM] * (len(rows_in) + len(held)) + [AN...  25.8 us
    pallas_call x2, Pallas kernels, second_phase(): pl.pallas_call(kernel, in_specs=[VMEM] * (len(parts) + len(sums) + len(he...  22.8 us
    all_to_all x1, blocking collectives, exchange(): return lax.all_to_all(cut, ROUTE_AXES, 0, 0, tiled=True).reshape(rows.shape)  15.2 us
    pallas_call x2, Pallas kernels, outer_products(): pl.pallas_call(kernel, in_specs=[VMEM] * (len(hiddens) + 1) + [ANY] * len...  11.2 us
    all_to_all x1, starting transfers between devices, exchange(): return lax.all_to_all(cut, ROUTE_AXES, 0, 0, tiled=True).reshape(rows.shape)  3.62 us
    ppermute x4, waiting for transfers between devices, from_peers(): lax.ppermute(value, axis, [(i, (i + hop) % size) for i in range(size)])  3.21 us
    ppermute x4, starting transfers between devices, from_peers(): lax.ppermute(value, axis, [(i, (i + hop) % size) for i in range(size)])  2.51 us
    pallas_call x1, Pallas kernels, route_rows(): pl.pallas_call(kernel, in_specs=[ANY] * 4, out_specs=[VMEM] * 2, out_shap...  2.01 us
  transfers between devices with their start and end apart: 5, of which 2 were waited for; matrix products, arithmetic and copies ran while one was open for 0% of the time, Pallas kernels for 40%

profile of v3, /device:TPU:0, one launch (start us, length us, event | category | flops | bytes accessed | tf_op | source)
XLA Modules:
  0.0 88.3 jit_solution(13500942636780664221)
XLA Ops:
  0.6 2.0 %route_rows.1 = (bf16[128,768]{1,0:T(8,128)(2,1)}, f32[128,16]{1,0:T(8,128)}) custom-call(bf16[16,768]{1,0:T(8,128)(2,1)} %tok_hbm.1, bf16[16,768]{1,0:T(8,128)(2,1)} %cot_hbm.1, s32[2,16]{1,0:T(2,128)} %bitcast.9, f32[2,16]{1,0:T(2,128)} %bitcast.10), custom_call_target="tpu_custom_call" | custom-call | tf_op jit(solution)/shard_map/route_rows/pallas_call | solution.py:79
  2.6 15.2 %all_to_all.10 = bf16[8,16,768]{2,1,0:T(8,128)(2,1)S(1)} all-to-all(bf16[8,16,768]{2,1,0:T(8,128)(2,1)} %bitcast.8), channel_id=1, replica_groups=mesh['dp'=2,'expert'=4,'tpin'=2,'tpout'=2] {'expert','tpout'}, dimensions={0} | all-to-all | bytes 393216 | tf_op jit(solution)/shard_map/all_to_all | solution.py:400
  17.9 12.9 %first_phase.2 = (f32[24,12288]{1,0:T(8,128)S(1)}, bf16[24,12288]{1,0:T(8,128)(2,1)S(1)}, bf16[1536,2048]{1,0:T(8,128)(2,1)S(1)}, bf16[24,1536]{1,0:T(8,128)(2,1)S(1)}, bf16[24,1536]{1,0:T(8,128)(2,1)S(1)}) custom-call(bf16[128,768]{1,0:T(8,128)(2,1)S(1)} %bitcast.7, bf16[1536,8192]{1,0:T(8,128)(2,1)} %refs_5_.3, bf16[1536,8192]{1,0:T(8,128)(2,1)} %refs_6_.1, ...), custom_call_target="tpu_custom_call" | custom-call | flops 9663676416 | bytes 37748736 | tf_op jit(solution)/shard_map/first_phase/pallas_call | solution.py:244
  30.8 1.6 %collective-permute-start = (bf16[24,12288]{1,0:T(8,128)(2,1)S(1)}, bf16[24,12288]{1,0:T(8,128)(2,1)S(1)}, u32[]{:S(2)}, u32[]{:S(2)}) collective-permute-start(bf16[24,12288]{1,0:T(8,128)(2,1)S(1)} %get-tuple-element.33), channel_id=1, source_target_pairs={{0,2},{2,0},{1,3},{3,1},{4,6},{6,4},{5,7},{7,5},{8,10},{10,8},{9,1... | collective-permute-start | bytes 1769480 | tf_op jit(solution)/shard_map/ppermute | solution.py:383
  32.4 12.9 %first_phase.3 = (f32[24,12288]{1,0:T(8,128)S(1)}, bf16[24,12288]{1,0:T(8,128)(2,1)S(1)}, bf16[1536,2048]{1,0:T(8,128)(2,1)S(1)}) custom-call(bf16[24,1536]{1,0:T(8,128)(2,1)S(1)} %get-tuple-element.28.refs_0_, bf16[24,1536]{1,0:T(8,128)(2,1)S(1)} %get-tuple-element.29.refs_1_.refs_2_, bf16[1536,8192]{1,0:T(8,128)(2,1)} %refs_5_.3, ...), custom_call_target="tpu_custom_call" | custom-call | flops 9663676416 | bytes 37748736 | tf_op jit(solution)/shard_map/first_phase/pallas_call | solution.py:244
  45.3 0.0 collective-permute-done
  45.3 0.1 fusion.1
  45.4 0.1 collective-permute-start.1
  45.5 0.7 collective-permute-start.2
  46.1 1.3 %collective-permute-done.1.refs_1_ = bf16[24,12288]{1,0:T(8,128)(2,1)S(1)} collective-permute-done((bf16[24,12288]{1,0:T(8,128)(2,1)S(1)}, bf16[24,12288]{1,0:T(8,128)(2,1)S(1)}, u32[]{:S(2)}, u32[]{:S(2)}) %collective-permute-start.1) | collective-permute-done | bytes 589856 | tf_op jit(solution)/shard_map/ppermute | solution.py:383
  47.5 11.1 %second_phase.2 = (bf16[24,4096]{1,0:T(8,128)(2,1)S(1)}, f32[24,1536]{1,0:T(8,128)S(1)}, f32[24,1536]{1,0:T(8,128)S(1)}) custom-call(f32[24,12288]{1,0:T(8,128)S(1)} %get-tuple-element.52.refs_0_, bf16[24,12288]{1,0:T(8,128)(2,1)S(1)} %collective-permute-done.1.refs_1_, bf16[1536,2048]{1,0:T(8,128)(2,1)S(1)} %get-tuple-element.34.refs_2_, ...), custom_call_target="tpu_custom_call" | custom-call | flops 9663676416 | bytes 37748736 | tf_op jit(solution)/shard_map/second_phase/pallas_call | solution.py:329
  58.5 2.8 %outer_products.2.refs_3_ = bf16[8192,1536]{1,0:T(8,128)(2,1)} custom-call(bf16[24,4096]{1,0:T(8,128)(2,1)S(1)} %get-tuple-element.37.refs_0_, bf16[24,1536]{1,0:T(8,128)(2,1)S(1)} %get-tuple-element.29.refs_1_.refs_2_), custom_call_target="tpu_custom_call" | custom-call | flops 1207959552 | bytes 4718592 | tf_op jit(solution)/shard_map/outer_products/pallas_call | solution.py:364
  61.3 0.0 collective-permute-done.2
  61.4 0.1 fusion
  61.5 0.2 collective-permute-start.3
  61.7 1.9 %collective-permute-done.3.refs_1_ = bf16[24,12288]{1,0:T(8,128)(2,1)S(1)} collective-permute-done((bf16[24,12288]{1,0:T(8,128)(2,1)S(1)}, bf16[24,12288]{1,0:T(8,128)(2,1)S(1)}, u32[]{:S(2)}, u32[]{:S(2)}) %collective-permute-start.3) | collective-permute-done | bytes 589856 | tf_op jit(solution)/shard_map/ppermute | solution.py:383
  63.6 11.7 %second_phase.3 = (bf16[24,4096]{1,0:T(8,128)(2,1)S(1)}, bf16[128,768]{1,0:T(8,128)(2,1)}) custom-call(f32[24,12288]{1,0:T(8,128)S(1)} %get-tuple-element.50.refs_0_, bf16[24,12288]{1,0:T(8,128)(2,1)S(1)} %collective-permute-done.3.refs_1_, f32[24,1536]{1,0:T(8,128)S(1)} %get-tuple-element.40.refs_2_, f32[24,1536]{1,0:T(8,128)S(1)} %get-tuple-element.41.refs_3_, ...), custom_call_target="tpu_custom_call" | custom-call | flops 9663676416 | bytes 37748736 | tf_op jit(solution)/shard_map/second_phase/pallas_call | solution.py:329
  75.3 3.6 %all-to-all-start.1 = ((bf16[8,16,768]{2,1,0:T(8,128)(2,1)}), bf16[8,16,768]{2,1,0:T(8,128)(2,1)S(1)}, u32[]{:S(2)}, u32[]{:S(2)}) async-start(bf16[8,16,768]{2,1,0:T(8,128)(2,1)} %bitcast.4), calls=%async_computation.1 | async-start | bytes 393216 | tf_op jit(solution)/shard_map/all_to_all | solution.py:400
  78.9 0.0 copy-start
  78.9 8.4 %outer_products.3 = bf16[8192,1536]{1,0:T(8,128)(2,1)} custom-call(bf16[24,4096]{1,0:T(8,128)(2,1)S(1)} %get-tuple-element.37.refs_0_, bf16[24,4096]{1,0:T(8,128)(2,1)S(1)} %get-tuple-element.47.refs_1_, bf16[24,1536]{1,0:T(8,128)(2,1)S(1)} %get-tuple-element.29.refs_1_.refs_2_, bf16[8192,1536]{1,0:T(8,128)(2,1)} %outer_products.2.refs_3_), custom_call_target="tpu_custom_call", output_to_operand_aliasing={{}: (3, {})} | custom-call | flops 5234491392 | bytes 20447232 | tf_op jit(solution)/shard_map/outer_products/pallas_call | solution.py:364
  87.3 0.0 all-to-all-done.1
  87.3 0.0 copy-done
  87.3 1.0 %combine_rows.1 = (bf16[16,768]{1,0:T(8,128)(2,1)}, bf16[16,768]{1,0:T(8,128)(2,1)}) custom-call(bf16[128,768]{1,0:T(8,128)(2,1)S(1)} %bitcast.6, f32[128,16]{1,0:T(8,128)S(1)} %copy-done), custom_call_target="tpu_custom_call" | custom-call | tf_op jit(solution)/shard_map/combine_rows/pallas_call | solution.py:111
Async XLA Ops:
  30.8 14.5 %collective-permute-start = (bf16[24,12288]{1,0:T(8,128)(2,1)S(1)}, bf16[24,12288]{1,0:T(8,128)(2,1)S(1)}, u32[]{:S(2)}, u32[]{:S(2)}) collective-permute-start(bf16[24,12288]{1,0:T(8,128)(2,1)S(1)} %get-tuple-element.33), channel_id=1, source_target_pairs={{0,2},{2,0},{1,3},{3,1},{4,6},{6,4},{5,7},{7,5},{8,10},{10,8},{9,1... | collective-permute-start | bytes 1769480 | tf_op jit(solution)/shard_map/ppermute | solution.py:383
  45.4 2.1 %collective-permute-start.1 = (bf16[24,12288]{1,0:T(8,128)(2,1)S(1)}, bf16[24,12288]{1,0:T(8,128)(2,1)S(1)}, u32[]{:S(2)}, u32[]{:S(2)}) collective-permute-start(bf16[24,12288]{1,0:T(8,128)(2,1)S(1)} %get-tuple-element.51), channel_id=1, source_target_pairs={{0,16},{16,0},{1,17},{17,1},{2,18},{18,2},{3,19},{19,3},{4,20},{20... | collective-permute-start | bytes 1769480 | tf_op jit(solution)/shard_map/ppermute | solution.py:383
  45.5 15.9 %collective-permute-start.2 = (bf16[24,12288]{1,0:T(8,128)(2,1)S(1)}, bf16[24,12288]{1,0:T(8,128)(2,1)S(1)}, u32[]{:S(2)}, u32[]{:S(2)}) collective-permute-start(bf16[24,12288]{1,0:T(8,128)(2,1)S(1)} %get-tuple-element.39), channel_id=1, source_target_pairs={{0,2},{2,0},{1,3},{3,1},{4,6},{6,4},{5,7},{7,5},{8,10},{10,8},{9,1... | collective-permute-start | bytes 1769480 | tf_op jit(solution)/shard_map/ppermute | solution.py:383
  61.5 2.1 %collective-permute-start.3 = (bf16[24,12288]{1,0:T(8,128)(2,1)S(1)}, bf16[24,12288]{1,0:T(8,128)(2,1)S(1)}, u32[]{:S(2)}, u32[]{:S(2)}) collective-permute-start(bf16[24,12288]{1,0:T(8,128)(2,1)S(1)} %get-tuple-element.49), channel_id=1, source_target_pairs={{0,16},{16,0},{1,17},{17,1},{2,18},{18,2},{3,19},{19,3},{4,20},{20... | collective-permute-start | bytes 1769480 | tf_op jit(solution)/shard_map/ppermute | solution.py:383
  75.3 12.0 %all-to-all-start.1 = ((bf16[8,16,768]{2,1,0:T(8,128)(2,1)}), bf16[8,16,768]{2,1,0:T(8,128)(2,1)S(1)}, u32[]{:S(2)}, u32[]{:S(2)}) async-start(bf16[8,16,768]{2,1,0:T(8,128)(2,1)} %bitcast.4), calls=%async_computation.1 | async-start | bytes 393216 | tf_op jit(solution)/shard_map/all_to_all | solution.py:400
  78.9 8.4 %copy-start = (f32[128,16]{1,0:T(8,128)S(1)}, f32[128,16]{1,0:T(8,128)}, u32[]{:S(2)}) copy-start(f32[128,16]{1,0:T(8,128)} %get-tuple-element.44.h) | copy-start | bytes 24580

commit v4 on v3

--- a/solution.py
+++ b/solution.py
@@ -37,63 +37,47 @@
     return pl.CostEstimate(flops=int(flops), bytes_accessed=int(nbytes), transcendentals=0)
 
 
-def route_rows(tokens, cotangent, ids, weights, devices, unit_cols):
-    tok_rows, feat = tokens.shape
+def route_rows(both, routes, devices, unit_cols):
+    tok_rows, feat = both.shape[0] // 2, both.shape[1]
     rows = devices * SLAB
-    top = ids.shape[0]
-
-    def kernel(tok_hbm, cot_hbm, ids_hbm, gw_hbm, send, home, tok, cot, ids_v, gw_v, sems):
-        pairs = ((ids_hbm, ids_v), (gw_hbm, gw_v), (tok_hbm, tok), (cot_hbm, cot))
-        copies = [
-            pltpu.make_async_copy(src, dst, sems.at[i]) for i, (src, dst) in enumerate(pairs)
-        ]
-        for copy in copies:
-            copy.start()
+    top = routes.shape[0] // 2
+
+    def kernel(both_ref, routes_ref, send, home):
         row = lax.broadcasted_iota(jnp.int32, (rows, tok_rows), 0)
         j = row % SLAB
-        want = row // SLAB * unit_cols // HID
+        want = (row // SLAB * unit_cols // HID).astype(jnp.float32)
         slot = jnp.where(j < 2 * CAP, j % CAP, -1)
         is_x = j < CAP
         earlier = lax.broadcasted_iota(jnp.int32, (tok_rows, tok_rows), 0)
         later = lax.broadcasted_iota(jnp.int32, (tok_rows, tok_rows), 1)
         before = jnp.where(earlier < later, 1.0, 0.0)
-        copies[0].wait()
-        copies[1].wait()
         hit = jnp.zeros((rows, tok_rows), jnp.float32)
         weight = jnp.zeros((rows, tok_rows), jnp.float32)
         for k in range(top):
-            same = ids_v[k : k + 1, :] == want
+            same = routes_ref[k : k + 1, :] == want
             hit += jnp.where(same, 1.0, 0.0)
-            weight += jnp.where(same, gw_v[k : k + 1, :], 0.0)
+            weight += jnp.where(same, routes_ref[top + k : top + k + 1, :], 0.0)
         rank = dot(hit, before)
         chosen = jnp.where(rank == slot.astype(jnp.float32), hit, 0.0)
         pick = chosen.astype(jnp.bfloat16)
         row_weight = jnp.sum(chosen * weight, axis=1, keepdims=True)
         home[...] = jnp.where(is_x, chosen * weight, chosen)
-        copies[2].wait()
-        x = dot(pick, tok[...])
-        copies[3].wait()
-        dy = row_weight * dot(pick, cot[...])
+        x = dot(pick, both_ref[:tok_rows, :])
+        dy = row_weight * dot(pick, both_ref[tok_rows:, :])
         send[...] = jnp.where(is_x[:, 0:1], x, dy).astype(jnp.bfloat16)
 
     return pl.pallas_call(
         kernel,
-        in_specs=[ANY] * 4,
+        in_specs=[VMEM] * 2,
         out_specs=[VMEM] * 2,
         out_shape=[
             jax.ShapeDtypeStruct((rows, feat), jnp.bfloat16),
             jax.ShapeDtypeStruct((rows, tok_rows), jnp.float32),
         ],
-        scratch_shapes=[
-            pltpu.VMEM(tokens.shape, tokens.dtype),
-            pltpu.VMEM(cotangent.shape, cotangent.dtype),
-            pltpu.VMEM(ids.shape, ids.dtype),
-            pltpu.VMEM(weights.shape, weights.dtype),
-            pltpu.SemaphoreType.DMA((4,)),
-        ],
-        compiler_params=params(63),
+        compiler_params=params(8),
+        cost_estimate=cost(2e10, 1 << 25),
         name="route_rows",
-    )(tokens, cotangent, ids, weights)
+    )(both, routes)
 
 
 def combine_rows(back, home, tok_rows):
@@ -391,9 +375,9 @@
     counts = (expert_count, outer_count)
     tok_rows, feat = tokens.shape
     unit_cols = w_gate.shape[1]
-    send, home = route_rows(
-        tokens, cotangent, expert_ids.T, gate_weights.T, expert_count * outer_count, unit_cols
-    )
+    both = jnp.concatenate([tokens, cotangent], 0)
+    routes = jnp.concatenate([expert_ids.T.astype(jnp.float32), gate_weights.T], 0)
+    send, home = route_rows(both, routes, expert_count * outer_count, unit_cols)
 
     def exchange(rows):
         cut = rows.reshape(expert_count * outer_count, SLAB, feat)
@@ -407,9 +391,12 @@
     rows_in = (exchange(send),)
     firsts, saved = [], []
     for n, (base, cols) in enumerate(chunks):
-        saves = [(0, base, keeps[n])]
+        if n == 0 and len(chunks) > 1:
+            held, saves = {0: (w_gate, 0, len(block_list(cols)))}, [(1, base, keeps[n])]
+        else:
+            held, saves = {}, [(0, base, keeps[n])]
         exact, rounded, *more = first_phase(
-            rows_in, weights, {}, saves, base, cols, counts
+            rows_in, weights, held, saves, base, cols, counts
         )
         for i, _, units in saves:
             saved.append({i: (more.pop(0), 0, len(block_list(units)))})

time: 88.7 us -> 87.6 us (0.988)
  Pallas kernels: 62.8 us -> 59.3 us
  other arithmetic: 0.24 us -> 2.52 us
    pallas_call x2, Pallas kernels: 25.8 us -> 24 us  [first_phase(): pl.pallas_call(kernel, in_specs=[VMEM] * (len(rows_in) + len(held)) + [AN...]
    pallas_call x1, Pallas kernels: 2.01 us -> 0.39 us  [route_rows(): pl.pallas_call(kernel, in_specs=[VMEM] * 2, out_specs=[VMEM] * 2, out_sha...]
    concatenate x0 -> x2, other arithmetic: none -> 1.6 us  [the longest x1 0.84 us: per_device(): jnp.concatenate([expert_ids.T.astype(jnp.float32), gate_weights.T], 0)]
where the time goes in v4:
time: 87.6 us; the launch traced here: 87.3 us
  Pallas kernels  59.3 us (68%)
  blocking collectives  15.3 us (17%)
  starting transfers between devices  6.14 us (7%)
  waiting for transfers between devices  3.2 us (4%)
  other arithmetic  2.52 us (3%)
    pallas_call x2, Pallas kernels, first_phase(): pl.pallas_call(kernel, in_specs=[VMEM] * (len(rows_in) + len(held)) + [AN...  24 us
    pallas_call x2, Pallas kernels, second_phase(): pl.pallas_call(kernel, in_specs=[VMEM] * (len(parts) + len(sums) + len(he...  22.8 us
    all_to_all x1, blocking collectives, exchange(): return lax.all_to_all(cut, ROUTE_AXES, 0, 0, tiled=True).reshape(rows.shape)  15.3 us
    pallas_call x2, Pallas kernels, outer_products(): pl.pallas_call(kernel, in_specs=[VMEM] * (len(hiddens) + 1) + [ANY] * len...  11.2 us
    all_to_all x1, starting transfers between devices, exchange(): return lax.all_to_all(cut, ROUTE_AXES, 0, 0, tiled=True).reshape(rows.shape)  3.62 us
    ppermute x4, waiting for transfers between devices, from_peers(): lax.ppermute(value, axis, [(i, (i + hop) % size) for i in range(size)])  3.2 us
    ppermute x4, starting transfers between devices, from_peers(): lax.ppermute(value, axis, [(i, (i + hop) % size) for i in range(size)])  2.52 us
  transfers between devices with their start and end apart: 5, of which 2 were waited for; matrix products, arithmetic and copies ran while one was open for 0% of the time, Pallas kernels for 40%

profile of v4, /device:TPU:0, one launch (start us, length us, event | category | flops | bytes accessed | tf_op | source)
XLA Modules:
  0.0 87.3 jit_solution(16573135453299912049)
XLA Ops:
  0.6 0.7 convert_bitcast_fusion
  1.3 0.8 pad_maximum_fusion.both_ref
  2.1 0.8 pad_maximum_fusion.1.routes_ref
  2.9 0.0 slice-start.3
  2.9 0.0 slice-start.4
  2.9 0.0 slice-start.5
  2.9 0.4 route_rows.1
  3.3 15.3 %all_to_all.10 = bf16[8,16,768]{2,1,0:T(8,128)(2,1)S(1)} all-to-all(bf16[8,16,768]{2,1,0:T(8,128)(2,1)S(1)} %bitcast.11), channel_id=1, replica_groups=mesh['dp'=2,'expert'=4,'tpin'=2,'tpout'=2] {'expert','tpout'}, dimensions={0} | all-to-all | bytes 393216 | tf_op jit(solution)/shard_map/all_to_all | solution.py:384
  18.6 0.0 slice-done
  18.6 0.0 slice-done.1
  18.6 0.0 slice-done.2
  18.6 0.0 slice-done.3
  18.6 0.0 slice-done.4
  18.7 11.1 %first_phase.2 = (f32[24,12288]{1,0:T(8,128)S(1)}, bf16[24,12288]{1,0:T(8,128)(2,1)S(1)}, bf16[1536,2048]{1,0:T(8,128)(2,1)S(1)}, bf16[24,1536]{1,0:T(8,128)(2,1)S(1)}, bf16[24,1536]{1,0:T(8,128)(2,1)S(1)}) custom-call(bf16[128,768]{1,0:T(8,128)(2,1)S(1)} %bitcast.10, bf16[1536,8192]{1,0:T(8,128)(2,1)S(1)} %bitcast.8, bf16[1536,8192]{1,0:T(8,128)(2,1)} %refs_6_.1, ...), custom_call_target="tpu_custom_call" | custom-call | flops 9663676416 | bytes 37748736 | tf_op jit(solution)/shard_map/first_phase/pallas_call | solution.py:228
  29.8 1.6 %collective-permute-start = (bf16[24,12288]{1,0:T(8,128)(2,1)S(1)}, bf16[24,12288]{1,0:T(8,128)(2,1)S(1)}, u32[]{:S(2)}, u32[]{:S(2)}) collective-permute-start(bf16[24,12288]{1,0:T(8,128)(2,1)S(1)} %get-tuple-element.33), channel_id=1, source_target_pairs={{0,2},{2,0},{1,3},{3,1},{4,6},{6,4},{5,7},{7,5},{8,10},{10,8},{9,1... | collective-permute-start | bytes 1769480 | tf_op jit(solution)/shard_map/ppermute | solution.py:367
  31.3 12.9 %first_phase.3 = (f32[24,12288]{1,0:T(8,128)S(1)}, bf16[24,12288]{1,0:T(8,128)(2,1)S(1)}, bf16[1536,2048]{1,0:T(8,128)(2,1)S(1)}) custom-call(bf16[24,1536]{1,0:T(8,128)(2,1)S(1)} %get-tuple-element.28.refs_0_, bf16[24,1536]{1,0:T(8,128)(2,1)S(1)} %get-tuple-element.29.refs_1_.refs_2_, bf16[1536,8192]{1,0:T(8,128)(2,1)} %refs_5_.3, ...), custom_call_target="tpu_custom_call" | custom-call | flops 9663676416 | bytes 37748736 | tf_op jit(solution)/shard_map/first_phase/pallas_call | solution.py:228
  44.2 0.0 collective-permute-done
  44.2 0.1 fusion.1
  44.4 0.1 collective-permute-start.1
  44.5 0.7 collective-permute-start.2
  45.1 1.3 %collective-permute-done.1.refs_1_ = bf16[24,12288]{1,0:T(8,128)(2,1)S(1)} collective-permute-done((bf16[24,12288]{1,0:T(8,128)(2,1)S(1)}, bf16[24,12288]{1,0:T(8,128)(2,1)S(1)}, u32[]{:S(2)}, u32[]{:S(2)}) %collective-permute-start.1) | collective-permute-done | bytes 589856 | tf_op jit(solution)/shard_map/ppermute | solution.py:367
  46.4 11.1 %second_phase.2 = (bf16[24,4096]{1,0:T(8,128)(2,1)S(1)}, f32[24,1536]{1,0:T(8,128)S(1)}, f32[24,1536]{1,0:T(8,128)S(1)}) custom-call(f32[24,12288]{1,0:T(8,128)S(1)} %get-tuple-element.52.refs_0_, bf16[24,12288]{1,0:T(8,128)(2,1)S(1)} %collective-permute-done.1.refs_1_, bf16[1536,2048]{1,0:T(8,128)(2,1)S(1)} %get-tuple-element.34.refs_2_, ...), custom_call_target="tpu_custom_call" | custom-call | flops 9663676416 | bytes 37748736 | tf_op jit(solution)/shard_map/second_phase/pallas_call | solution.py:313
  57.5 2.8 %outer_products.2.refs_3_ = bf16[8192,1536]{1,0:T(8,128)(2,1)} custom-call(bf16[24,4096]{1,0:T(8,128)(2,1)S(1)} %get-tuple-element.37.refs_0_, bf16[24,1536]{1,0:T(8,128)(2,1)S(1)} %get-tuple-element.29.refs_1_.refs_2_), custom_call_target="tpu_custom_call" | custom-call | flops 1207959552 | bytes 4718592 | tf_op jit(solution)/shard_map/outer_products/pallas_call | solution.py:348
  60.3 0.0 collective-permute-done.2
  60.3 0.1 fusion
  60.5 0.2 collective-permute-start.3
  60.7 1.9 %collective-permute-done.3.refs_1_ = bf16[24,12288]{1,0:T(8,128)(2,1)S(1)} collective-permute-done((bf16[24,12288]{1,0:T(8,128)(2,1)S(1)}, bf16[24,12288]{1,0:T(8,128)(2,1)S(1)}, u32[]{:S(2)}, u32[]{:S(2)}) %collective-permute-start.3) | collective-permute-done | bytes 589856 | tf_op jit(solution)/shard_map/ppermute | solution.py:367
  62.5 11.7 %second_phase.3 = (bf16[24,4096]{1,0:T(8,128)(2,1)S(1)}, bf16[128,768]{1,0:T(8,128)(2,1)}) custom-call(f32[24,12288]{1,0:T(8,128)S(1)} %get-tuple-element.50.refs_0_, bf16[24,12288]{1,0:T(8,128)(2,1)S(1)} %collective-permute-done.3.refs_1_, f32[24,1536]{1,0:T(8,128)S(1)} %get-tuple-element.40.refs_2_, f32[24,1536]{1,0:T(8,128)S(1)} %get-tuple-element.41.refs_3_, ...), custom_call_target="tpu_custom_call" | custom-call | flops 9663676416 | bytes 37748736 | tf_op jit(solution)/shard_map/second_phase/pallas_call | solution.py:313
  74.3 3.6 %all-to-all-start.1 = ((bf16[8,16,768]{2,1,0:T(8,128)(2,1)}), bf16[8,16,768]{2,1,0:T(8,128)(2,1)S(1)}, u32[]{:S(2)}, u32[]{:S(2)}) async-start(bf16[8,16,768]{2,1,0:T(8,128)(2,1)} %bitcast.4), calls=%async_computation.1 | async-start | bytes 393216 | tf_op jit(solution)/shard_map/all_to_all | solution.py:384
  77.9 8.4 %outer_products.3 = bf16[8192,1536]{1,0:T(8,128)(2,1)} custom-call(bf16[24,4096]{1,0:T(8,128)(2,1)S(1)} %get-tuple-element.37.refs_0_, bf16[24,4096]{1,0:T(8,128)(2,1)S(1)} %get-tuple-element.47.refs_1_, bf16[24,1536]{1,0:T(8,128)(2,1)S(1)} %get-tuple-element.29.refs_1_.refs_2_, bf16[8192,1536]{1,0:T(8,128)(2,1)} %outer_products.2.refs_3_), custom_call_target="tpu_custom_call", output_to_operand_aliasing={{}: (3, {})} | custom-call | flops 5234491392 | bytes 20447232 | tf_op jit(solution)/shard_map/outer_products/pallas_call | solution.py:348
  86.3 0.0 all-to-all-done.1
  86.3 1.0 %combine_rows.1 = (bf16[16,768]{1,0:T(8,128)(2,1)}, bf16[16,768]{1,0:T(8,128)(2,1)}) custom-call(bf16[128,768]{1,0:T(8,128)(2,1)S(1)} %bitcast.9, f32[128,16]{1,0:T(8,128)S(1)} %get-tuple-element.44.h), custom_call_target="tpu_custom_call" | custom-call | tf_op jit(solution)/shard_map/combine_rows/pallas_call | solution.py:95
  (5 shorter events, 0.0 us)
Async XLA Ops:
  2.1 16.5 %slice-start = ((s8[25165824]{0:T(1024)(128)(4,1)}), s8[4194304]{0:T(1024)(128)(4,1)S(1)}, s32[]{:S(2)}) async-start(s8[25165824]{0:T(1024)(128)(4,1)} %bitcast.7), calls=%async_computation.2 | async-start | bytes 8388608
  2.9 15.7 %slice-start.1 = ((s8[25165824]{0:T(1024)(128)(4,1)}), s8[4194304]{0:T(1024)(128)(4,1)S(1)}, s32[]{:S(2)}) async-start(s8[25165824]{0:T(1024)(128)(4,1)} %bitcast.7), calls=%async_computation.3 | async-start | bytes 8388608
  2.9 15.7 %slice-start.2 = ((s8[25165824]{0:T(1024)(128)(4,1)}), s8[4194304]{0:T(1024)(128)(4,1)S(1)}, s32[]{:S(2)}) async-start(s8[25165824]{0:T(1024)(128)(4,1)} %bitcast.7), calls=%async_computation.4 | async-start | bytes 8388608
  2.9 15.7 %slice-start.3 = ((s8[25165824]{0:T(1024)(128)(4,1)}), s8[4194304]{0:T(1024)(128)(4,1)S(1)}, s32[]{:S(2)}) async-start(s8[25165824]{0:T(1024)(128)(4,1)} %bitcast.7), calls=%async_computation.5 | async-start | bytes 8388608
  2.9 15.7 %slice-start.4 = ((s8[25165824]{0:T(1024)(128)(4,1)}), s8[4194304]{0:T(1024)(128)(4,1)S(1)}, s32[]{:S(2)}) async-start(s8[25165824]{0:T(1024)(128)(4,1)} %bitcast.7), calls=%async_computation.6 | async-start | bytes 8388608
  2.9 15.7 %slice-start.5 = ((s8[25165824]{0:T(1024)(128)(4,1)}), s8[4194304]{0:T(1024)(128)(4,1)S(1)}, s32[]{:S(2)}) async-start(s8[25165824]{0:T(1024)(128)(4,1)} %bitcast.7), calls=%async_computation.7 | async-start | bytes 8388608
  29.8 14.5 %collective-permute-start = (bf16[24,12288]{1,0:T(8,128)(2,1)S(1)}, bf16[24,12288]{1,0:T(8,128)(2,1)S(1)}, u32[]{:S(2)}, u32[]{:S(2)}) collective-permute-start(bf16[24,12288]{1,0:T(8,128)(2,1)S(1)} %get-tuple-element.33), channel_id=1, source_target_pairs={{0,2},{2,0},{1,3},{3,1},{4,6},{6,4},{5,7},{7,5},{8,10},{10,8},{9,1... | collective-permute-start | bytes 1769480 | tf_op jit(solution)/shard_map/ppermute | solution.py:367
  44.4 2.1 %collective-permute-start.1 = (bf16[24,12288]{1,0:T(8,128)(2,1)S(1)}, bf16[24,12288]{1,0:T(8,128)(2,1)S(1)}, u32[]{:S(2)}, u32[]{:S(2)}) collective-permute-start(bf16[24,12288]{1,0:T(8,128)(2,1)S(1)} %get-tuple-element.51), channel_id=1, source_target_pairs={{0,16},{16,0},{1,17},{17,1},{2,18},{18,2},{3,19},{19,3},{4,20},{20... | collective-permute-start | bytes 1769480 | tf_op jit(solution)/shard_map/ppermute | solution.py:367
  44.5 15.9 %collective-permute-start.2 = (bf16[24,12288]{1,0:T(8,128)(2,1)S(1)}, bf16[24,12288]{1,0:T(8,128)(2,1)S(1)}, u32[]{:S(2)}, u32[]{:S(2)}) collective-permute-start(bf16[24,12288]{1,0:T(8,128)(2,1)S(1)} %get-tuple-element.39), channel_id=1, source_target_pairs={{0,2},{2,0},{1,3},{3,1},{4,6},{6,4},{5,7},{7,5},{8,10},{10,8},{9,1... | collective-permute-start | bytes 1769480 | tf_op jit(solution)/shard_map/ppermute | solution.py:367
  60.5 2.1 %collective-permute-start.3 = (bf16[24,12288]{1,0:T(8,128)(2,1)S(1)}, bf16[24,12288]{1,0:T(8,128)(2,1)S(1)}, u32[]{:S(2)}, u32[]{:S(2)}) collective-permute-start(bf16[24,12288]{1,0:T(8,128)(2,1)S(1)} %get-tuple-element.49), channel_id=1, source_target_pairs={{0,16},{16,0},{1,17},{17,1},{2,18},{18,2},{3,19},{19,3},{4,20},{20... | collective-permute-start | bytes 1769480 | tf_op jit(solution)/shard_map/ppermute | solution.py:367
  74.3 12.0 %all-to-all-start.1 = ((bf16[8,16,768]{2,1,0:T(8,128)(2,1)}), bf16[8,16,768]{2,1,0:T(8,128)(2,1)S(1)}, u32[]{:S(2)}, u32[]{:S(2)}) async-start(bf16[8,16,768]{2,1,0:T(8,128)(2,1)} %bitcast.4), calls=%async_computation.1 | async-start | bytes 393216 | tf_op jit(solution)/shard_map/all_to_all | solution.py:384

commit v5 on v4

--- a/solution.py
+++ b/solution.py
@@ -139,9 +139,9 @@
         if copy is not None:
             copy.start()
 
-    def open(self):
+    def open(self, order):
         for step in range(DEPTH):
-            for which in range(3):
+            for which in order:
                 self.start(which, step)
 
     def take(self, which, step):
@@ -202,11 +202,12 @@
         slots = {i: refs.pop(0) for i in live}
         sems = refs.pop(0)
         stream = Stream(sources, slots, sems, base, blocks, stays)
-        stream.open()
+        order = (0, 2, 1)
+        stream.open(order)
         if opening:
             spread(rows_refs[0], x_all, dy_all, counts)
         for step, (at, width) in enumerate(blocks):
-            for i in range(3):
+            for i in order:
                 weight = stream.take(i, step)[...]
                 if i < 2:
                     part = dot(x_all[...], weight)
@@ -258,7 +259,7 @@
         sems, gate_grad, up_grad, *rest = refs
         acc = rest[:2] if last else outs
         stream = Stream(sources, slots, sems, base, blocks, stays)
-        stream.open()
+        stream.open(order)
         for at, width in blocks:
             gate, up, hidden_grad = [
                 sum(p[:, i * cols + at : i * cols + at + width].astype(jnp.float32) for p in part_refs)

time: 87.6 us -> 87.3 us (level)
  no operation moved by 1% of the time
where the time goes in v5:
time: 87.3 us; the launch traced here: 87 us
  Pallas kernels  59.1 us (68%)
  blocking collectives  15.3 us (18%)
  starting transfers between devices  6.28 us (7%)
  waiting for transfers between devices  3.08 us (4%)
  other arithmetic  2.52 us (3%)
    pallas_call x2, Pallas kernels, first_phase(): pl.pallas_call(kernel, in_specs=[VMEM] * (len(rows_in) + len(held)) + [AN...  23.7 us
    pallas_call x2, Pallas kernels, second_phase(): pl.pallas_call(kernel, in_specs=[VMEM] * (len(parts) + len(sums) + len(he...  22.8 us
    all_to_all x1, blocking collectives, exchange(): return lax.all_to_all(cut, ROUTE_AXES, 0, 0, tiled=True).reshape(rows.shape)  15.3 us
    pallas_call x2, Pallas kernels, outer_products(): pl.pallas_call(kernel, in_specs=[VMEM] * (len(hiddens) + 1) + [ANY] * len...  11.2 us
    all_to_all x1, starting transfers between devices, exchange(): return lax.all_to_all(cut, ROUTE_AXES, 0, 0, tiled=True).reshape(rows.shape)  3.63 us
    ppermute x4, waiting for transfers between devices, from_peers(): lax.ppermute(value, axis, [(i, (i + hop) % size) for i in range(size)])  3.07 us
    ppermute x4, starting transfers between devices, from_peers(): lax.ppermute(value, axis, [(i, (i + hop) % size) for i in range(size)])  2.65 us
  transfers between devices with their start and end apart: 5, of which 2 were waited for; matrix products, arithmetic and copies ran while one was open for 0% of the time, Pallas kernels for 40%

profile of v5, /device:TPU:0, one launch (start us, length us, event | category | flops | bytes accessed | tf_op | source)
XLA Modules:
  0.0 87.0 jit_solution(4023945188412837779)
XLA Ops:
  0.6 0.7 convert_bitcast_fusion
  1.3 0.8 pad_maximum_fusion.both_ref
  2.1 0.8 pad_maximum_fusion.1.routes_ref
  2.9 0.0 slice-start.3
  2.9 0.0 slice-start.4
  2.9 0.0 slice-start.5
  2.9 0.4 route_rows.1
  3.3 15.3 %all_to_all.10 = bf16[8,16,768]{2,1,0:T(8,128)(2,1)S(1)} all-to-all(bf16[8,16,768]{2,1,0:T(8,128)(2,1)S(1)} %bitcast.11), channel_id=1, replica_groups=mesh['dp'=2,'expert'=4,'tpin'=2,'tpout'=2] {'expert','tpout'}, dimensions={0} | all-to-all | bytes 393216 | tf_op jit(solution)/shard_map/all_to_all | solution.py:385
  18.6 0.0 slice-done
  18.6 0.0 slice-done.1
  18.6 0.0 slice-done.2
  18.6 0.0 slice-done.3
  18.6 0.0 slice-done.4
  18.7 11.0 %first_phase.2 = (f32[24,12288]{1,0:T(8,128)S(1)}, bf16[24,12288]{1,0:T(8,128)(2,1)S(1)}, bf16[1536,2048]{1,0:T(8,128)(2,1)S(1)}, bf16[24,1536]{1,0:T(8,128)(2,1)S(1)}, bf16[24,1536]{1,0:T(8,128)(2,1)S(1)}) custom-call(bf16[128,768]{1,0:T(8,128)(2,1)S(1)} %bitcast.10, bf16[1536,8192]{1,0:T(8,128)(2,1)S(1)} %bitcast.8, bf16[1536,8192]{1,0:T(8,128)(2,1)} %refs_6_.1, ...), custom_call_target="tpu_custom_call" | custom-call | flops 9663676416 | bytes 37748736 | tf_op jit(solution)/shard_map/first_phase/pallas_call | solution.py:229
  29.6 1.6 %collective-permute-start = (bf16[24,12288]{1,0:T(8,128)(2,1)S(1)}, bf16[24,12288]{1,0:T(8,128)(2,1)S(1)}, u32[]{:S(2)}, u32[]{:S(2)}) collective-permute-start(bf16[24,12288]{1,0:T(8,128)(2,1)S(1)} %get-tuple-element.33), channel_id=1, source_target_pairs={{0,2},{2,0},{1,3},{3,1},{4,6},{6,4},{5,7},{7,5},{8,10},{10,8},{9,1... | collective-permute-start | bytes 1769480 | tf_op jit(solution)/shard_map/ppermute | solution.py:368
  31.2 12.8 %first_phase.3 = (f32[24,12288]{1,0:T(8,128)S(1)}, bf16[24,12288]{1,0:T(8,128)(2,1)S(1)}, bf16[1536,2048]{1,0:T(8,128)(2,1)S(1)}) custom-call(bf16[24,1536]{1,0:T(8,128)(2,1)S(1)} %get-tuple-element.28.refs_0_, bf16[24,1536]{1,0:T(8,128)(2,1)S(1)} %get-tuple-element.29.refs_1_.refs_2_, bf16[1536,8192]{1,0:T(8,128)(2,1)} %refs_5_.3, ...), custom_call_target="tpu_custom_call" | custom-call | flops 9663676416 | bytes 37748736 | tf_op jit(solution)/shard_map/first_phase/pallas_call | solution.py:229
  44.0 0.0 collective-permute-done
  44.0 0.1 fusion.1
  44.1 0.1 collective-permute-start.1
  44.2 0.8 collective-permute-start.2
  45.0 1.2 %collective-permute-done.1.refs_1_ = bf16[24,12288]{1,0:T(8,128)(2,1)S(1)} collective-permute-done((bf16[24,12288]{1,0:T(8,128)(2,1)S(1)}, bf16[24,12288]{1,0:T(8,128)(2,1)S(1)}, u32[]{:S(2)}, u32[]{:S(2)}) %collective-permute-start.1) | collective-permute-done | bytes 589856 | tf_op jit(solution)/shard_map/ppermute | solution.py:368
  46.2 11.1 %second_phase.2 = (bf16[24,4096]{1,0:T(8,128)(2,1)S(1)}, f32[24,1536]{1,0:T(8,128)S(1)}, f32[24,1536]{1,0:T(8,128)S(1)}) custom-call(f32[24,12288]{1,0:T(8,128)S(1)} %get-tuple-element.52.refs_0_, bf16[24,12288]{1,0:T(8,128)(2,1)S(1)} %collective-permute-done.1.refs_1_, bf16[1536,2048]{1,0:T(8,128)(2,1)S(1)} %get-tuple-element.34.refs_2_, ...), custom_call_target="tpu_custom_call" | custom-call | flops 9663676416 | bytes 37748736 | tf_op jit(solution)/shard_map/second_phase/pallas_call | solution.py:314
  57.3 2.8 %outer_products.2.refs_3_ = bf16[8192,1536]{1,0:T(8,128)(2,1)} custom-call(bf16[24,4096]{1,0:T(8,128)(2,1)S(1)} %get-tuple-element.37.refs_0_, bf16[24,1536]{1,0:T(8,128)(2,1)S(1)} %get-tuple-element.29.refs_1_.refs_2_), custom_call_target="tpu_custom_call" | custom-call | flops 1207959552 | bytes 4718592 | tf_op jit(solution)/shard_map/outer_products/pallas_call | solution.py:349
  60.1 0.0 collective-permute-done.2
  60.1 0.1 fusion
  60.2 0.2 collective-permute-start.3
  60.4 1.9 %collective-permute-done.3.refs_1_ = bf16[24,12288]{1,0:T(8,128)(2,1)S(1)} collective-permute-done((bf16[24,12288]{1,0:T(8,128)(2,1)S(1)}, bf16[24,12288]{1,0:T(8,128)(2,1)S(1)}, u32[]{:S(2)}, u32[]{:S(2)}) %collective-permute-start.3) | collective-permute-done | bytes 589856 | tf_op jit(solution)/shard_map/ppermute | solution.py:368
  62.3 11.7 %second_phase.3 = (bf16[24,4096]{1,0:T(8,128)(2,1)S(1)}, bf16[128,768]{1,0:T(8,128)(2,1)}) custom-call(f32[24,12288]{1,0:T(8,128)S(1)} %get-tuple-element.50.refs_0_, bf16[24,12288]{1,0:T(8,128)(2,1)S(1)} %collective-permute-done.3.refs_1_, f32[24,1536]{1,0:T(8,128)S(1)} %get-tuple-element.40.refs_2_, f32[24,1536]{1,0:T(8,128)S(1)} %get-tuple-element.41.refs_3_, ...), custom_call_target="tpu_custom_call" | custom-call | flops 9663676416 | bytes 37748736 | tf_op jit(solution)/shard_map/second_phase/pallas_call | solution.py:314
  74.0 3.6 %all-to-all-start.1 = ((bf16[8,16,768]{2,1,0:T(8,128)(2,1)}), bf16[8,16,768]{2,1,0:T(8,128)(2,1)S(1)}, u32[]{:S(2)}, u32[]{:S(2)}) async-start(bf16[8,16,768]{2,1,0:T(8,128)(2,1)} %bitcast.4), calls=%async_computation.1 | async-start | bytes 393216 | tf_op jit(solution)/shard_map/all_to_all | solution.py:385
  77.6 8.4 %outer_products.3 = bf16[8192,1536]{1,0:T(8,128)(2,1)} custom-call(bf16[24,4096]{1,0:T(8,128)(2,1)S(1)} %get-tuple-element.37.refs_0_, bf16[24,4096]{1,0:T(8,128)(2,1)S(1)} %get-tuple-element.47.refs_1_, bf16[24,1536]{1,0:T(8,128)(2,1)S(1)} %get-tuple-element.29.refs_1_.refs_2_, bf16[8192,1536]{1,0:T(8,128)(2,1)} %outer_products.2.refs_3_), custom_call_target="tpu_custom_call", output_to_operand_aliasing={{}: (3, {})} | custom-call | flops 5234491392 | bytes 20447232 | tf_op jit(solution)/shard_map/outer_products/pallas_call | solution.py:349
  86.0 0.0 all-to-all-done.1
  86.0 1.0 %combine_rows.1 = (bf16[16,768]{1,0:T(8,128)(2,1)}, bf16[16,768]{1,0:T(8,128)(2,1)}) custom-call(bf16[128,768]{1,0:T(8,128)(2,1)S(1)} %bitcast.9, f32[128,16]{1,0:T(8,128)S(1)} %get-tuple-element.44.h), custom_call_target="tpu_custom_call" | custom-call | tf_op jit(solution)/shard_map/combine_rows/pallas_call | solution.py:95
  (5 shorter events, 0.0 us)
Async XLA Ops:
  2.1 16.5 %slice-start = ((s8[25165824]{0:T(1024)(128)(4,1)}), s8[4194304]{0:T(1024)(128)(4,1)S(1)}, s32[]{:S(2)}) async-start(s8[25165824]{0:T(1024)(128)(4,1)} %bitcast.7), calls=%async_computation.2 | async-start | bytes 8388608
  2.9 15.7 %slice-start.1 = ((s8[25165824]{0:T(1024)(128)(4,1)}), s8[4194304]{0:T(1024)(128)(4,1)S(1)}, s32[]{:S(2)}) async-start(s8[25165824]{0:T(1024)(128)(4,1)} %bitcast.7), calls=%async_computation.3 | async-start | bytes 8388608
  2.9 15.7 %slice-start.2 = ((s8[25165824]{0:T(1024)(128)(4,1)}), s8[4194304]{0:T(1024)(128)(4,1)S(1)}, s32[]{:S(2)}) async-start(s8[25165824]{0:T(1024)(128)(4,1)} %bitcast.7), calls=%async_computation.4 | async-start | bytes 8388608
  2.9 15.7 %slice-start.3 = ((s8[25165824]{0:T(1024)(128)(4,1)}), s8[4194304]{0:T(1024)(128)(4,1)S(1)}, s32[]{:S(2)}) async-start(s8[25165824]{0:T(1024)(128)(4,1)} %bitcast.7), calls=%async_computation.5 | async-start | bytes 8388608
  2.9 15.7 %slice-start.4 = ((s8[25165824]{0:T(1024)(128)(4,1)}), s8[4194304]{0:T(1024)(128)(4,1)S(1)}, s32[]{:S(2)}) async-start(s8[25165824]{0:T(1024)(128)(4,1)} %bitcast.7), calls=%async_computation.6 | async-start | bytes 8388608
  2.9 15.7 %slice-start.5 = ((s8[25165824]{0:T(1024)(128)(4,1)}), s8[4194304]{0:T(1024)(128)(4,1)S(1)}, s32[]{:S(2)}) async-start(s8[25165824]{0:T(1024)(128)(4,1)} %bitcast.7), calls=%async_computation.7 | async-start | bytes 8388608
  29.6 14.3 %collective-permute-start = (bf16[24,12288]{1,0:T(8,128)(2,1)S(1)}, bf16[24,12288]{1,0:T(8,128)(2,1)S(1)}, u32[]{:S(2)}, u32[]{:S(2)}) collective-permute-start(bf16[24,12288]{1,0:T(8,128)(2,1)S(1)} %get-tuple-element.33), channel_id=1, source_target_pairs={{0,2},{2,0},{1,3},{3,1},{4,6},{6,4},{5,7},{7,5},{8,10},{10,8},{9,1... | collective-permute-start | bytes 1769480 | tf_op jit(solution)/shard_map/ppermute | solution.py:368
  44.1 2.1 %collective-permute-start.1 = (bf16[24,12288]{1,0:T(8,128)(2,1)S(1)}, bf16[24,12288]{1,0:T(8,128)(2,1)S(1)}, u32[]{:S(2)}, u32[]{:S(2)}) collective-permute-start(bf16[24,12288]{1,0:T(8,128)(2,1)S(1)} %get-tuple-element.51), channel_id=1, source_target_pairs={{0,16},{16,0},{1,17},{17,1},{2,18},{18,2},{3,19},{19,3},{4,20},{20... | collective-permute-start | bytes 1769480 | tf_op jit(solution)/shard_map/ppermute | solution.py:368
  44.2 15.9 %collective-permute-start.2 = (bf16[24,12288]{1,0:T(8,128)(2,1)S(1)}, bf16[24,12288]{1,0:T(8,128)(2,1)S(1)}, u32[]{:S(2)}, u32[]{:S(2)}) collective-permute-start(bf16[24,12288]{1,0:T(8,128)(2,1)S(1)} %get-tuple-element.39), channel_id=1, source_target_pairs={{0,2},{2,0},{1,3},{3,1},{4,6},{6,4},{5,7},{7,5},{8,10},{10,8},{9,1... | collective-permute-start | bytes 1769480 | tf_op jit(solution)/shard_map/ppermute | solution.py:368
  60.2 2.1 %collective-permute-start.3 = (bf16[24,12288]{1,0:T(8,128)(2,1)S(1)}, bf16[24,12288]{1,0:T(8,128)(2,1)S(1)}, u32[]{:S(2)}, u32[]{:S(2)}) collective-permute-start(bf16[24,12288]{1,0:T(8,128)(2,1)S(1)} %get-tuple-element.49), channel_id=1, source_target_pairs={{0,16},{16,0},{1,17},{17,1},{2,18},{18,2},{3,19},{19,3},{4,20},{20... | collective-permute-start | bytes 1769480 | tf_op jit(solution)/shard_map/ppermute | solution.py:368
  74.0 12.0 %all-to-all-start.1 = ((bf16[8,16,768]{2,1,0:T(8,128)(2,1)}), bf16[8,16,768]{2,1,0:T(8,128)(2,1)S(1)}, u32[]{:S(2)}, u32[]{:S(2)}) async-start(bf16[8,16,768]{2,1,0:T(8,128)(2,1)} %bitcast.4), calls=%async_computation.1 | async-start | bytes 393216 | tf_op jit(solution)/shard_map/all_to_all | solution.py:385
